TPU v7x, 128 devices: a whole 4x4x4 slice. The times are simulated.
128 devices in a mesh: pool: 16 (over x, z), head: 8 (over y, core).
Axes of the slice: x: 4, y: 4, z: 4, core: 2. Of those that a mesh axis runs over, the one named last changes fastest.
Arguments:
- light_query: bfloat16 [8192, 8192], P('pool', 'head'), may hold values from -6 to 6
- light_key: bfloat16 [8192, 8192], P('pool', 'head'), may hold values from -0.5 to 0.5
- light_value: bfloat16 [8192, 8192], P('pool', 'head'), may hold values from -40 to 40
- light_gate: bfloat16 [8192, 8192], P('pool', 'head'), may hold values from -6 to 6
- decay_rate: float32 [64], P('head'), may hold values from 0.001 to 0.06
- norm_gain: float32 [8192], P('head'), may hold values from 0.5 to 1.5
- state_store: float32 [64, 64, 128, 128], P('pool', 'head'), may hold values from -6 to 6
- state_slot: int32 [64, 64], P('pool', 'head'), may hold values from 0 to 63, as said below
- soft_query: bfloat16 [8192, 8192], P('pool', 'head'), may hold values from -120 to 120
- soft_pair: bfloat16 [8192, 2048], P('pool', 'head'), may hold values from -6 to 6
- kv_store: bfloat16 [2048, 8, 128, 256], P(('pool', 'head')), may hold values from -8 to 8
- page_holder: int32 [64, 32, 1], P('pool'), may hold values from 0 to 127; in each aligned block of 128 rows (0 to 127, 128 to 255, ..., all dimensions but the last counted through in order) at most 2 rows name the same one
- page_local: int32 [64, 32], P('pool'), may hold values from 0 to 15
- prefix_len: int32 [64], P('pool'), may hold values from 1 to 4096, as said below
Outputs:
- light_out: bfloat16 [8192, 8192], P('pool', 'head')
- new_state: float32 [64, 64, 128, 128], P('pool', 'head')
- soft_out: bfloat16 [8192, 8192], P('pool', 'head')
Inputs may be any that keep to these rules, and one draw needn't show every extreme that they name: `state_slot`: A slot names holder row slot // 4. In one device's block of 4 requests by 8 heads at most 4 slots lie on one holder row, and every block has a holder row with exactly 4. `page_holder`: devices are numbered pool index times 8 plus head index. `prefix_len`: some request has the full 32 pages of 128 tokens in every draw; page slots past a request's length are not read.
All inputs are finite; a program needn't handle non-finite values.
Results may differ from a plain program's by a relative error of at most 0.0047.
Values may be sent and summed in bfloat16 or wider, within the bound.
A program may use at most 128 MiB of HBM per device.

v0:
```python
import math

import jax
import jax.numpy as jnp
from jax import lax
from jax.sharding import PartitionSpec as P


def lightning(queries, keys_in, values_in, rates_in, initial):
    length = queries.shape[1]
    highest = lax.Precision.HIGHEST
    offsets = jnp.arange(length).astype(jnp.float32)
    spacing = offsets[:, None] - offsets[None, :]
    weights = (
        jnp.exp(-rates_in[:, None, None] * jnp.maximum(spacing, 0.0)[None])
        * (spacing >= 0.0).astype(jnp.float32)[None]
    )
    scores = (
        jnp.einsum("rthd,rshd->rhts", queries, keys_in, preferred_element_type=jnp.float32)
        * weights[None]
    )
    rounded = scores.astype(jnp.bfloat16)
    inside = jnp.einsum("rhts,rshe->rthe", rounded, values_in, preferred_element_type=jnp.float32)
    leading = jnp.exp(-rates_in[None, :] * (offsets[:, None] + 1.0))
    carried = jnp.einsum(
        "rthd,rhde->rthe",
        queries.astype(jnp.float32) * leading[None, :, :, None],
        initial,
        precision=highest,
    )
    trailing = jnp.exp(-rates_in[None, :] * (length - 1.0 - offsets[:, None]))
    updated = jnp.exp(-rates_in * length)[None, :, None, None] * initial + jnp.einsum(
        "rshd,rshe->rhde",
        keys_in.astype(jnp.float32) * trailing[None, :, :, None],
        values_in.astype(jnp.float32),
        precision=highest,
    )
    return (inside + carried, updated)


def attend(query_rows, suffix_kv, prefix_kv, length):
    suffix = query_rows.shape[0]
    key_heads = prefix_kv.shape[1]
    head_width = prefix_kv.shape[-1] // 2
    group_size = query_rows.shape[1] // head_width // key_heads
    grouped = (
        query_rows.reshape(suffix, key_heads, group_size, head_width)
        .transpose(1, 2, 0, 3)
        .reshape(key_heads, group_size * suffix, head_width)
    )
    earlier = prefix_kv.transpose(1, 0, 2, 3).reshape(key_heads, -1, 2 * head_width)
    recent = suffix_kv.reshape(suffix, key_heads, 2 * head_width).transpose(1, 0, 2)
    joined = jnp.concatenate([earlier, recent], axis=1)
    cached_count = earlier.shape[1]
    column = jnp.arange(cached_count + suffix)
    moment = jnp.arange(group_size * suffix) % suffix
    allowed = jnp.where(
        column[None, :] < cached_count,
        column[None, :] < length,
        column[None, :] - cached_count <= moment[:, None],
    )
    temper = 1.0 / math.sqrt(head_width)

    def per_head(operands):
        group_query, group_pair = operands
        scores = (
            jnp.dot(group_query, group_pair[:, :head_width].T, preferred_element_type=jnp.float32)
            * temper
        )
        scores = jnp.where(allowed, scores, -1e30)
        highest = jnp.max(scores, axis=1, keepdims=True)
        lifted = jnp.exp(scores - highest)
        totals = jnp.sum(lifted, axis=1, keepdims=True)
        mixed = jnp.dot(
            lifted.astype(jnp.bfloat16),
            group_pair[:, head_width:],
            preferred_element_type=jnp.float32,
        )
        return mixed / totals

    result = lax.map(per_head, (grouped, joined))
    return (
        result.reshape(key_heads, group_size, suffix, head_width)
        .transpose(2, 0, 1, 3)
        .reshape(suffix, key_heads * group_size * head_width)
        .astype(jnp.bfloat16)
    )


def plan_lists(holder_ids, local_ids, holder_count, capacity):
    matches = (holder_ids[:, None] == jnp.arange(holder_count, dtype=jnp.int32)[None, :]).astype(
        jnp.int32
    )
    before = jnp.cumsum(matches, axis=0) - matches
    ranking = jnp.sum(before * matches, axis=1)
    chosen = matches.T[:, None, :] * (
        ranking[None, None, :] == jnp.arange(capacity, dtype=jnp.int32)[None, :, None]
    ).astype(jnp.int32)
    requests_out = jnp.sum(chosen * local_ids[None, None, :], axis=2)
    return (requests_out, holder_ids * capacity + ranking)


def state_entries(slot_rows, stored_states, group_heads):
    flat_slots = slot_rows.reshape(-1)
    within = jnp.tile(jnp.arange(group_heads, dtype=jnp.int32), flat_slots.shape[0] // group_heads)
    return (flat_slots // stored_states, flat_slots % stored_states * group_heads + within)


def body(
    light_query,
    light_key,
    light_value,
    light_gate,
    decay_rate,
    norm_gain,
    state_store,
    state_slot,
    soft_query,
    soft_pair,
    kv_store,
    page_holder,
    page_local,
    prefix_len,
):
    owners = lax.axis_size("pool")
    groups = lax.axis_size("head")
    holders = owners * groups
    requests = prefix_len.shape[0]
    group_heads = decay_rate.shape[0]
    head_width = state_store.shape[-1]
    stored_states = state_store.shape[0]
    stored_pages = kv_store.shape[0]
    key_heads = kv_store.shape[1] // groups
    page_tokens = kv_store.shape[2]
    max_pages = page_local.shape[1]
    suffix = light_query.shape[0] // requests
    state_capacity = max(2, 2 * requests * group_heads // owners)
    page_capacity = max(2, 2 * requests * max_pages // holders)
    state_holders, state_locals = state_entries(state_slot, stored_states, group_heads)
    state_asks, state_picks = plan_lists(state_holders, state_locals, owners, state_capacity)
    page_asks, page_picks = plan_lists(
        page_holder.reshape(-1), page_local.reshape(-1), holders, page_capacity
    )
    state_served = lax.all_to_all(state_asks, "pool", split_axis=0, concat_axis=0, tiled=True)
    page_served = lax.all_to_all(
        page_asks, ("pool", "head"), split_axis=0, concat_axis=0, tiled=True
    )
    flat_states = state_store.reshape(stored_states * group_heads, head_width, head_width)
    outgoing = jnp.take(flat_states, state_served.reshape(-1), axis=0).reshape(
        owners, state_capacity, head_width, head_width
    )
    arrived = lax.all_to_all(outgoing, "pool", split_axis=0, concat_axis=0, tiled=True)
    initial = jnp.take(
        arrived.reshape(owners * state_capacity, head_width, head_width), state_picks, axis=0
    ).reshape(requests, group_heads, head_width, head_width)
    page_rows = kv_store.reshape(stored_pages * groups, key_heads, page_tokens, 2 * head_width)
    target_head = jnp.arange(holders, dtype=jnp.int32) % groups
    wanted = page_served * groups + target_head[:, None]
    outgoing_pages = jnp.take(page_rows, wanted.reshape(-1), axis=0).reshape(
        holders, page_capacity, key_heads, page_tokens, 2 * head_width
    )
    arrived_pages = lax.all_to_all(
        outgoing_pages, ("pool", "head"), split_axis=0, concat_axis=0, tiled=True
    )
    prefix = jnp.take(
        arrived_pages.reshape(holders * page_capacity, key_heads, page_tokens, 2 * head_width),
        page_picks,
        axis=0,
    ).reshape(requests, max_pages, key_heads, page_tokens, 2 * head_width)
    output, updated = lightning(
        light_query.reshape(requests, suffix, group_heads, head_width),
        light_key.reshape(requests, suffix, group_heads, head_width),
        light_value.reshape(requests, suffix, group_heads, head_width),
        decay_rate,
        initial,
    )
    squares = jnp.sum(output * output, axis=(2, 3))
    totals = lax.psum(squares, "head")
    factor = lax.rsqrt(totals / (groups * group_heads * head_width) + 1e-06)
    normed = (
        output.reshape(requests * suffix, group_heads * head_width)
        * factor.reshape(-1, 1)
        * norm_gain
        * jax.nn.sigmoid(light_gate.astype(jnp.float32))
    )
    light_out = normed.astype(jnp.bfloat16)

    def one_request(position):
        first_row = position * suffix
        return attend(
            lax.dynamic_slice_in_dim(soft_query, first_row, suffix, 0),
            lax.dynamic_slice_in_dim(soft_pair, first_row, suffix, 0),
            prefix[position],
            prefix_len[position],
        )

    soft_out = lax.map(one_request, jnp.arange(requests, dtype=jnp.int32)).reshape(
        requests * suffix, group_heads * head_width
    )
    return (light_out, updated, soft_out)


def solution(mesh):
    return jax.shard_map(
        body,
        mesh=mesh,
        in_specs=(
            P("pool", "head"),
            P("pool", "head"),
            P("pool", "head"),
            P("pool", "head"),
            P("head"),
            P("head"),
            P("pool", "head", None, None),
            P("pool", "head"),
            P("pool", "head"),
            P("pool", "head"),
            P(("pool", "head"), None, None, None),
            P("pool", None, None),
            P("pool", None),
            P("pool"),
        ),
        out_specs=(P("pool", "head"), P("pool", "head", None, None), P("pool", "head")),
        check_vma=False,
    )
```

profile of v0, /device:TPU:98, one launch (start us, length us, event | category | flops | bytes accessed | tf_op | source)
XLA Modules:
  0.0 522.3 jit_solution(18230965027737760770)
XLA Ops:
  14.4 9.5 %all-to-all-start.2 = ((s32[128,1,2]{2,1,0:T(1,128)}), s32[128,1,2]{2,1,0:T(1,128)S(1)}, u32[]{:S(2)}, u32[]{:S(2)}) async-start(s32[128,1,2]{2,1,0:T(1,128)} %copy.89), calls=%async_computation.2 | async-start | bytes 131072 | tf_op jit(solution)/shard_map/all_to_all | solution.py:145
  32.2 7.0 %all-to-all-start.1 = ((f32[16,4,128,128]{3,2,1,0:T(8,128)}), f32[16,4,128,128]{3,2,1,0:T(8,128)}, u32[]{:S(2)}, u32[]{:S(2)}) async-start(f32[16,4,128,128]{3,2,1,0:T(8,128)} %broadcast_select_fusion.2), calls=%async_computation.1 | async-start | bytes 8388608 | tf_op jit(solution)/shard_map/all_to_all | solution.py:152
  39.9 12.7 %gather_fusion.2 = bf16[256,128,256]{2,1,0:T(8,128)(2,1)} fusion(bf16[128,128,256]{2,1,0:T(8,128)(2,1)} %bitcast.105, s32[1024]{0:T(1024)S(1)} %pad_clamp_fusion.1), kind=kCustom, calls=%fused_computation.2 | custom fusion | bytes 33555456 | tf_op jit(solution)/shard_map/jit(_take)/gather | solution.py:159
  52.6 14.1 %broadcast_select_fusion = bf16[128,2,1,128,256]{4,3,1,2,0:T(8,128)(2,1)} fusion(bf16[128,2,1,128,256]{4,3,1,2,0:T(8,128)(2,1)} %bitcast.103, pred[128,2]{1,0:T(8,128)(4,1)S(1)} %copy.91), kind=kLoop, calls=%fused_computation.27 | loop fusion | flops 8388608 | bytes 33554688 | tf_op jit(solution)/shard_map/jit(_take)/select_n | solution.py:159
  66.7 27.2 %all-to-all-done.1 = f32[16,4,128,128]{3,2,1,0:T(8,128)} async-done(((f32[16,4,128,128]{3,2,1,0:T(8,128)}), f32[16,4,128,128]{3,2,1,0:T(8,128)}, u32[]{:S(2)}, u32[]{:S(2)}) %all-to-all-start.1) | async-done | bytes 4194336 | tf_op jit(solution)/shard_map/all_to_all | solution.py:152
  93.9 21.7 %all-to-all-start.3 = ((bf16[128,2,1,128,256]{4,3,1,2,0:T(8,128)(2,1)}), bf16[128,2,1,128,256]{4,3,1,2,0:T(8,128)(2,1)}, u32[]{:S(2)}, u32[]{:S(2)}) async-start(bf16[128,2,1,128,256]{4,3,1,2,0:T(8,128)(2,1)} %broadcast_select_fusion), calls=%async_computation.3 | async-start | bytes 33554432 | tf_op jit(solution)/shard_map/all_to_all | solution.py:162
  127.2 7.4 %multiply_reduce_fusion = (f32[4,128]{1,0:T(4,128)S(1)}, f32[4,128,8,128]{1,3,2,0:T(8,128)}) fusion(f32[128,8]{0,1:T(8,128)S(1)} %get-tuple-element.164, bf16[4,128,8,128]{3,2,1,0:T(8,128)(2,1)} %bitcast.114, f32[4,8,128,128]{3,2,1,0:T(8,128)S(1)} %bitcast.108, pred[4,8]{1,0:T(4,128)(4,1)S(1)} %compare_and_fusion.3, f32[4,8,128,128]{2,3,1,0:T(8,128)} %fusion.32), kind=kOutput, calls=%fused_computation.38 | convolution fusion | flops 808451584 | bytes 7346208 | tf_op jit(solution)/shard_map/rthd,rhde->rthe/dot_general | solution.py:25
  137.5 179.1 %psum.7 = f32[4,128]{1,0:T(4,128)S(1)} all-reduce(f32[4,128]{1,0:T(4,128)S(1)} %get-tuple-element.167), channel_id=1, replica_groups=mesh['pool'=16,'head'=8] {'head'}, use_global_device_ids=true, to_apply=%region_4.5 | all-reduce | flops 512 | bytes 4096 | tf_op jit(solution)/shard_map/psum | solution.py:178
  322.5 37.6 %all-to-all-done.3 = bf16[128,2,1,128,256]{4,3,1,2,0:T(8,128)(2,1)} async-done(((bf16[128,2,1,128,256]{4,3,1,2,0:T(8,128)(2,1)}), bf16[128,2,1,128,256]{4,3,1,2,0:T(8,128)(2,1)}, u32[]{:S(2)}, u32[]{:S(2)}) %all-to-all-start.3) | async-done | bytes 16777248 | tf_op jit(solution)/shard_map/all_to_all | solution.py:162
  360.1 12.3 %gather_fusion.3 = bf16[128,128,256]{2,1,0:T(8,128)(2,1)} fusion(bf16[256,128,256]{2,1,0:T(8,128)(2,1)} %bitcast.28, s32[1024]{0:T(1024)S(1)} %pad_clamp_fusion), kind=kCustom, calls=%fused_computation.3 | custom fusion | bytes 16777728 | tf_op jit(solution)/shard_map/jit(_take)/gather | solution.py:165
  372.4 7.5 %broadcast_select_fusion.1 = bf16[4,32,1,128,256]{4,3,2,1,0:T(8,128)(2,1)} fusion(bf16[4,32,1,128,256]{4,3,2,1,0:T(8,128)(2,1)} %bitcast.106, pred[4,32]{1,0:T(4,128)(4,1)S(1)} %compare_and_fusion.1), kind=kLoop, calls=%fused_computation.28 | loop fusion | flops 4194304 | bytes 16777344 | tf_op jit(solution)/shard_map/jit(_take)/select_n | solution.py:165
  379.9 140.8 %while.16 = (s32[]{:T(128)}, bf16[4,128,1024]{2,1,0:T(8,128)(2,1)}, s32[4]{0:T(128)S(1)}, s32[4]{0:T(128)S(1)}, bf16[512,1024]{1,0:T(8,128)(2,1)}, /*index=5*/bf...) while((s32[]{:T(128)}, bf16[4,128,1024]{2,1,0:T(8,128)(2,1)}, ...), condition=%wide.region_11.12_spmd, body=%wide.region_8.11_spmd.sunk | while | flops 2258125312 | bytes 75123736 | solution.py:197
  388.5 8.6 %fusion.72 = (f32[1024]{0:T(1024)S(1)}, f32[1024,4224]{1,0:T(8,128)}) fusion(bf16[1024,128]{1,0:T(8,128)(2,1)S(1)} %bitcast.116, bf16[4224,256]{1,0:T(8,128)(2,1)S(1)} %maximum_bitcast_fusion.2, s32[1024]{0:T(1024)S(1)} %add_select_fusion.3, s32[4224]{0:T(1024)S(1)} %iota_add_fusion.2, pred[4224]{0:T(1024)(128)(4,1)S(1)} %get-tuple-element.218, ...), kind=kOutput, calls=%fused_computation.128.clone.1 | convolution fusion | flops 1128922112 | bytes 18683904 | tf_op jit(solution)/shard_map/while/body/eval_jaxpr/while/body/eval_jaxpr/dot_general | solution.py:67
  397.1 8.3 %fusion.73 = f32[1024]{0:T(1024)S(1)} fusion(f32[1024,4224]{1,0:T(8,128)} %get-tuple-element.220, f32[1024]{0:T(1024)S(1)} %get-tuple-element.221), kind=kLoop, calls=%fused_computation.6.clone.1 | loop fusion | flops 8649728 | bytes 17309696 | tf_op jit(solution)/shard_map/while/body/eval_jaxpr/while/body/eval_jaxpr/reduce_sum | solution.py:73
  405.4 8.6 %fusion.74 = bf16[1024,128]{1,0:T(8,128)(2,1)S(1)} fusion(f32[1024,4224]{1,0:T(8,128)} %get-tuple-element.220, f32[1024]{0:T(1024)S(1)} %get-tuple-element.221, bf16[4224,256]{1,0:T(8,128)(2,1)} %copy-done.2, f32[1024]{0:T(1024)S(1)} %fusion.73), kind=kOutput, calls=%fused_computation.12.clone.1 | convolution fusion | flops 1116209152 | bytes 18653184 | tf_op jit(solution)/shard_map/while/body/eval_jaxpr/while/body/eval_jaxpr/dot_general | solution.py:74
  423.7 8.6 %fusion.72 = (f32[1024]{0:T(1024)S(1)}, f32[1024,4224]{1,0:T(8,128)}) fusion(bf16[1024,128]{1,0:T(8,128)(2,1)S(1)} %bitcast.116, bf16[4224,256]{1,0:T(8,128)(2,1)S(1)} %maximum_bitcast_fusion.2, s32[1024]{0:T(1024)S(1)} %add_select_fusion.3, s32[4224]{0:T(1024)S(1)} %iota_add_fusion.2, pred[4224]{0:T(1024)(128)(4,1)S(1)} %get-tuple-element.218, ...), kind=kOutput, calls=%fused_computation.128.clone.1 | convolution fusion | flops 1128922112 | bytes 18683904 | tf_op jit(solution)/shard_map/while/body/eval_jaxpr/while/body/eval_jaxpr/dot_general | solution.py:67
  432.3 8.3 %fusion.73 = f32[1024]{0:T(1024)S(1)} fusion(f32[1024,4224]{1,0:T(8,128)} %get-tuple-element.220, f32[1024]{0:T(1024)S(1)} %get-tuple-element.221), kind=kLoop, calls=%fused_computation.6.clone.1 | loop fusion | flops 8649728 | bytes 17309696 | tf_op jit(solution)/shard_map/while/body/eval_jaxpr/while/body/eval_jaxpr/reduce_sum | solution.py:73
  440.6 8.6 %fusion.74 = bf16[1024,128]{1,0:T(8,128)(2,1)S(1)} fusion(f32[1024,4224]{1,0:T(8,128)} %get-tuple-element.220, f32[1024]{0:T(1024)S(1)} %get-tuple-element.221, bf16[4224,256]{1,0:T(8,128)(2,1)} %copy-done.2, f32[1024]{0:T(1024)S(1)} %fusion.73), kind=kOutput, calls=%fused_computation.12.clone.1 | convolution fusion | flops 1116209152 | bytes 18653184 | tf_op jit(solution)/shard_map/while/body/eval_jaxpr/while/body/eval_jaxpr/dot_general | solution.py:74
  458.9 8.6 %fusion.72 = (f32[1024]{0:T(1024)S(1)}, f32[1024,4224]{1,0:T(8,128)}) fusion(bf16[1024,128]{1,0:T(8,128)(2,1)S(1)} %bitcast.116, bf16[4224,256]{1,0:T(8,128)(2,1)S(1)} %maximum_bitcast_fusion.2, s32[1024]{0:T(1024)S(1)} %add_select_fusion.3, s32[4224]{0:T(1024)S(1)} %iota_add_fusion.2, pred[4224]{0:T(1024)(128)(4,1)S(1)} %get-tuple-element.218, ...), kind=kOutput, calls=%fused_computation.128.clone.1 | convolution fusion | flops 1128922112 | bytes 18683904 | tf_op jit(solution)/shard_map/while/body/eval_jaxpr/while/body/eval_jaxpr/dot_general | solution.py:67
  467.5 8.3 %fusion.73 = f32[1024]{0:T(1024)S(1)} fusion(f32[1024,4224]{1,0:T(8,128)} %get-tuple-element.220, f32[1024]{0:T(1024)S(1)} %get-tuple-element.221), kind=kLoop, calls=%fused_computation.6.clone.1 | loop fusion | flops 8649728 | bytes 17309696 | tf_op jit(solution)/shard_map/while/body/eval_jaxpr/while/body/eval_jaxpr/reduce_sum | solution.py:73
  475.8 8.6 %fusion.74 = bf16[1024,128]{1,0:T(8,128)(2,1)S(1)} fusion(f32[1024,4224]{1,0:T(8,128)} %get-tuple-element.220, f32[1024]{0:T(1024)S(1)} %get-tuple-element.221, bf16[4224,256]{1,0:T(8,128)(2,1)} %copy-done.2, f32[1024]{0:T(1024)S(1)} %fusion.73), kind=kOutput, calls=%fused_computation.12.clone.1 | convolution fusion | flops 1116209152 | bytes 18653184 | tf_op jit(solution)/shard_map/while/body/eval_jaxpr/while/body/eval_jaxpr/dot_general | solution.py:74
  494.1 8.6 %fusion.72 = (f32[1024]{0:T(1024)S(1)}, f32[1024,4224]{1,0:T(8,128)}) fusion(bf16[1024,128]{1,0:T(8,128)(2,1)S(1)} %bitcast.116, bf16[4224,256]{1,0:T(8,128)(2,1)S(1)} %maximum_bitcast_fusion.2, s32[1024]{0:T(1024)S(1)} %add_select_fusion.3, s32[4224]{0:T(1024)S(1)} %iota_add_fusion.2, pred[4224]{0:T(1024)(128)(4,1)S(1)} %get-tuple-element.218, ...), kind=kOutput, calls=%fused_computation.128.clone.1 | convolution fusion | flops 1128922112 | bytes 18683904 | tf_op jit(solution)/shard_map/while/body/eval_jaxpr/while/body/eval_jaxpr/dot_general | solution.py:67
  502.7 8.3 %fusion.73 = f32[1024]{0:T(1024)S(1)} fusion(f32[1024,4224]{1,0:T(8,128)} %get-tuple-element.220, f32[1024]{0:T(1024)S(1)} %get-tuple-element.221), kind=kLoop, calls=%fused_computation.6.clone.1 | loop fusion | flops 8649728 | bytes 17309696 | tf_op jit(solution)/shard_map/while/body/eval_jaxpr/while/body/eval_jaxpr/reduce_sum | solution.py:73
  511.0 8.6 %fusion.74 = bf16[1024,128]{1,0:T(8,128)(2,1)S(1)} fusion(f32[1024,4224]{1,0:T(8,128)} %get-tuple-element.220, f32[1024]{0:T(1024)S(1)} %get-tuple-element.221, bf16[4224,256]{1,0:T(8,128)(2,1)} %copy-done.2, f32[1024]{0:T(1024)S(1)} %fusion.73), kind=kOutput, calls=%fused_computation.12.clone.1 | convolution fusion | flops 1116209152 | bytes 18653184 | tf_op jit(solution)/shard_map/while/body/eval_jaxpr/while/body/eval_jaxpr/dot_general | solution.py:74
  (161 shorter events, 72.6 us)
Async XLA Ops:
  0.6 24.3 %copy-start = (f32[4,8,128,128]{3,2,1,0:T(8,128)S(1)}, f32[4,8,128,128]{3,2,1,0:T(8,128)}, u32[]{:S(2)}) copy-start(f32[4,8,128,128]{3,2,1,0:T(8,128)} %param.22) | copy-start | bytes 6291460
  2.8 11.6 %all-to-all-start = ((s32[16,1,4]{2,1,0:T(1,128)}), s32[16,1,4]{2,1,0:T(1,128)S(1)}, u32[]{:S(2)}, u32[]{:S(2)}) async-start(s32[16,1,4]{2,1,0:T(1,128)} %copy.81), calls=%async_computation | async-start | bytes 16384 | tf_op jit(solution)/shard_map/all_to_all | solution.py:144
  14.4 17.7 %all-to-all-start.2 = ((s32[128,1,2]{2,1,0:T(1,128)}), s32[128,1,2]{2,1,0:T(1,128)S(1)}, u32[]{:S(2)}, u32[]{:S(2)}) async-start(s32[128,1,2]{2,1,0:T(1,128)} %copy.89), calls=%async_computation.2 | async-start | bytes 131072 | tf_op jit(solution)/shard_map/all_to_all | solution.py:145
  32.2 61.7 %all-to-all-start.1 = ((f32[16,4,128,128]{3,2,1,0:T(8,128)}), f32[16,4,128,128]{3,2,1,0:T(8,128)}, u32[]{:S(2)}, u32[]{:S(2)}) async-start(f32[16,4,128,128]{3,2,1,0:T(8,128)} %broadcast_select_fusion.2), calls=%async_computation.1 | async-start | bytes 8388608 | tf_op jit(solution)/shard_map/all_to_all | solution.py:152
  66.7 48.9 %copy-start.9 = (s32[4,8]{1,0:T(4,128)S(1)}, s32[4,8]{1,0:T(4,128)}, u32[]{:S(2)}) copy-start(s32[4,8]{1,0:T(4,128)} %param.23) | copy-start | bytes 388
  66.7 49.3 %copy-start.7 = (bf16[512,1024]{1,0:T(8,128)(2,1)S(1)}, bf16[512,1024]{1,0:T(8,128)(2,1)}, u32[]{:S(2)}) copy-start(bf16[512,1024]{1,0:T(8,128)(2,1)} %param.16) | copy-start | bytes 3145732
  93.9 266.2 %all-to-all-start.3 = ((bf16[128,2,1,128,256]{4,3,1,2,0:T(8,128)(2,1)}), bf16[128,2,1,128,256]{4,3,1,2,0:T(8,128)(2,1)}, u32[]{:S(2)}, u32[]{:S(2)}) async-start(bf16[128,2,1,128,256]{4,3,1,2,0:T(8,128)(2,1)} %broadcast_select_fusion), calls=%async_computation.3 | async-start | bytes 33554432 | tf_op jit(solution)/shard_map/all_to_all | solution.py:162
  115.6 1.2 copy-start.8
  116.3 4.5 copy-start.4
  117.1 2.4 copy-start.11
  119.4 4.9 copy-start.3
  316.7 4.2 copy-start.5
  316.7 4.2 copy-start.6
  316.7 4.2 copy-start.10
  372.4 7.5 %copy-start.12 = (s32[4]{0:T(128)S(1)}, s32[4]{0:T(128)}, u32[]{:S(2)}) copy-start(s32[4]{0:T(128)} %param.29) | copy-start | bytes 52
  388.5 8.6 %copy-start.2 = (bf16[4224,256]{1,0:T(8,128)(2,1)}, bf16[4224,256]{1,0:T(8,128)(2,1)S(1)}, u32[]{:S(2)}) copy-start(bf16[4224,256]{1,0:T(8,128)(2,1)S(1)} %maximum_bitcast_fusion.2) | copy-start | bytes 6488068 | tf_op jit(solution)/shard_map/while
  423.7 8.6 %copy-start.2 = (bf16[4224,256]{1,0:T(8,128)(2,1)}, bf16[4224,256]{1,0:T(8,128)(2,1)S(1)}, u32[]{:S(2)}) copy-start(bf16[4224,256]{1,0:T(8,128)(2,1)S(1)} %maximum_bitcast_fusion.2) | copy-start | bytes 6488068 | tf_op jit(solution)/shard_map/while
  458.9 8.6 %copy-start.2 = (bf16[4224,256]{1,0:T(8,128)(2,1)}, bf16[4224,256]{1,0:T(8,128)(2,1)S(1)}, u32[]{:S(2)}) copy-start(bf16[4224,256]{1,0:T(8,128)(2,1)S(1)} %maximum_bitcast_fusion.2) | copy-start | bytes 6488068 | tf_op jit(solution)/shard_map/while
  494.1 8.6 %copy-start.2 = (bf16[4224,256]{1,0:T(8,128)(2,1)}, bf16[4224,256]{1,0:T(8,128)(2,1)S(1)}, u32[]{:S(2)}) copy-start(bf16[4224,256]{1,0:T(8,128)(2,1)S(1)} %maximum_bitcast_fusion.2) | copy-start | bytes 6488068 | tf_op jit(solution)/shard_map/while
  520.7 1.6 copy-start.1
where the time goes:
time: 524 us; the launch traced here: 522 us
  blocking collectives  179 us (34%)
  matrix products  84 us (16%)
  local copies, waits for them, and re-layouts  68.7 us (13%)
  other arithmetic  68.5 us (13%)
  waiting for transfers between devices  65.3 us (12%)
  starting transfers between devices  45.2 us (9%)
  loops' own time  10.4 us (2%)
    psum x1, blocking collectives, body(): totals = lax.psum(squares, 'head')  179 us
    all_to_all x1, waiting for transfers between devices, body(): lax.all_to_all(outgoing_pages, ('pool', 'head'), split_axis=0, concat_axi...  37.6 us
    dot_general x4, matrix products, per_head(): jnp.dot(lifted.astype(jnp.bfloat16), group_pair[:, head_width:], preferre...  34.6 us
    dot_general x4, matrix products, per_head(): jnp.dot(group_query, group_pair[:, :head_width].T, preferred_element_type...  34.3 us
    reduce_sum x4, other arithmetic, per_head(): totals = jnp.sum(lifted, axis=1, keepdims=True)  33.2 us
    all_to_all x1, waiting for transfers between devices, body(): lax.all_to_all(outgoing, 'pool', split_axis=0, concat_axis=0, tiled=True)  27.2 us
    all_to_all x1, starting transfers between devices, body(): lax.all_to_all(outgoing_pages, ('pool', 'head'), split_axis=0, concat_axi...  21.7 us
    select_n x2, other arithmetic, body(): jnp.take(page_rows, wanted.reshape(-1), axis=0)  14.1 us
  transfers between devices with their start and end apart: 4, of which 3 were waited for; matrix products, arithmetic and copies ran while one was open for 13% of the time, Pallas kernels for 0%

commit v1 on v0

--- a/solution.py
+++ b/solution.py
@@ -1,8 +1,11 @@
+import functools
 import math
 
 import jax
 import jax.numpy as jnp
 from jax import lax
+from jax.experimental import pallas as pl
+from jax.experimental.pallas import tpu as pltpu
 from jax.sharding import PartitionSpec as P
 
 
@@ -106,7 +109,7 @@
     return (flat_slots // stored_states, flat_slots % stored_states * group_heads + within)
 
 
-def body(
+def general_body(
     light_query,
     light_key,
     light_value,
@@ -200,6 +203,432 @@
     return (light_out, updated, soft_out)
 
 
+MESH = pl.DeviceIdType.MESH
+LANES = 128
+CHUNKS = 8
+ROW_CAP = 11
+STATE_CAP = 4
+LOG2E = 1.4426950408889634
+
+
+def wait_bytes(ref, sem):
+    pltpu.make_async_copy(ref, ref, sem).wait()
+
+
+def fused_kernel(
+    row_cap,
+    table,
+    rates,
+    q_in,
+    k_in,
+    v_in,
+    gate_in,
+    gain_in,
+    store_in,
+    soft_q,
+    pair_in,
+    kv_ref,
+    light_out,
+    state_out,
+    soft_out,
+    a_buf,
+    a_cur,
+    s_buf,
+    r_buf,
+    r_cur,
+    key_buf,
+    val_buf,
+    st_send,
+    st_recv,
+    mix,
+    sq_send,
+    sq_recv,
+    q_cat,
+    acc,
+    top,
+    a_send,
+    a_recv,
+    b_send,
+    b_recv,
+    keep_sems,
+    st_sems,
+    sq_sems,
+):
+    f32, bf16 = jnp.float32, jnp.bfloat16
+    tokens = LANES // CHUNKS
+    keys = 32 * tokens
+    pool, head = lax.axis_index("pool"), lax.axis_index("head")
+    px, pz = pool // 4, lax.rem(pool, 4)
+    hy, hc = head // 2, lax.rem(head, 2)
+    heads_to = [lax.rem(hy + k // 2, 4) * 2 + lax.rem(hc + k % 2, 2) for k in range(1, 8)]
+    pools_to = [lax.rem(px + k // 4, 4) * 4 + lax.rem(pz + k % 4, 4) for k in range(1, 16)]
+    pick_at, place_at, len_at = 0, 16 * row_cap, 16 * row_cap + 128
+    st_pick_at, st_place_at = len_at + 4, len_at + 4 + 64
+
+    barrier = pltpu.get_barrier_semaphore()
+    for d in heads_to:
+        pl.semaphore_signal(barrier, inc=1, device_id={"head": d}, device_id_type=MESH)
+    for d in pools_to:
+        pl.semaphore_signal(barrier, inc=1, device_id={"pool": d}, device_id_type=MESH)
+    pl.semaphore_wait(barrier, 22)
+
+    def send_store(t, carry):
+        part = pl.ds(pl.multiple_of(t * tokens, tokens), tokens)
+        for d in heads_to:
+            pltpu.make_async_remote_copy(
+                kv_ref.at[:, d, part, :],
+                a_buf.at[t, pl.ds(head * 16, 16)],
+                a_send.at[t],
+                a_recv.at[t],
+                device_id={"head": d},
+                device_id_type=MESH,
+            ).start()
+        pltpu.make_async_copy(
+            kv_ref.at[:, head, part, :], a_buf.at[t, pl.ds(head * 16, 16)], a_recv.at[t]
+        ).start()
+        return carry
+
+    lax.fori_loop(0, CHUNKS, send_store, 0)
+
+    def pack_state(i, carry):
+        for c in range(STATE_CAP):
+            st_send[i * STATE_CAP + c] = store_in[table[st_pick_at + i * STATE_CAP + c]].astype(bf16)
+        return carry
+
+    lax.fori_loop(0, 16, pack_state, 0)
+    mine_st = pl.ds(pool * STATE_CAP, STATE_CAP)
+    for d in pools_to:
+        pltpu.make_async_remote_copy(
+            st_send.at[pl.ds(d * STATE_CAP, STATE_CAP)],
+            st_recv.at[mine_st],
+            st_sems.at[0],
+            st_sems.at[1],
+            device_id={"pool": d},
+            device_id_type=MESH,
+        ).start()
+    pltpu.make_async_copy(st_send.at[mine_st], st_recv.at[mine_st], st_sems.at[1]).start()
+
+    temper = LOG2E / math.sqrt(LANES)
+    val_buf[:, LANES:] = jnp.ones((keys, LANES), bf16)
+    row_i = lax.broadcasted_iota(jnp.int32, (LANES, LANES), 0)
+    col_i = lax.broadcasted_iota(jnp.int32, (LANES, LANES), 1)
+
+    def rows_of(r):
+        return pl.ds(pl.multiple_of(r * LANES, LANES), LANES)
+
+    def open_softmax(e, carry):
+        r, h = e // 8, lax.rem(e, 8)
+        q = soft_q[rows_of(r), rows_of(h)]
+        q_cat[r, rows_of(h), :] = q
+        k = pair_in[rows_of(r), :LANES]
+        v = pair_in[rows_of(r), LANES:]
+        s = lax.dot_general(q, k, (((1,), (1,)), ((), ())), preferred_element_type=f32) * temper
+        s = jnp.where(col_i <= row_i, s, -1e30)
+        peak = jnp.max(s, axis=1, keepdims=True)
+        p = jnp.exp2(s - peak).astype(bf16)
+        acc[r, rows_of(h), :LANES] = jnp.dot(p, v, preferred_element_type=f32)
+        acc[r, rows_of(h), LANES:] = jnp.dot(p, jnp.ones((LANES, LANES), bf16), preferred_element_type=f32)
+        top[r, rows_of(h), :] = jnp.broadcast_to(peak, (LANES, LANES))
+        return carry
+
+    lax.fori_loop(0, 32, open_softmax, 0)
+
+    lane = lax.broadcasted_iota(jnp.int32, (1, keys), 1)
+
+    def attend_chunk(t):
+        wait_bytes(r_buf.at[t, pl.ds(0, 15 * row_cap)], b_recv.at[t])
+        r_cur[...] = r_buf[t]
+        spot = (lane // tokens) * LANES + t * tokens + lax.rem(lane, tokens)
+
+        def one_request(r, carry):
+            for p in range(32):
+                block = r_cur[table[place_at + r * 32 + p]]
+                key_buf[p * tokens : (p + 1) * tokens, :] = block[:, :LANES]
+                val_buf[p * tokens : (p + 1) * tokens, :LANES] = block[:, LANES:]
+            bias = jnp.where(spot < table[len_at + r], 0.0, -1e30).astype(f32)
+
+            def one_block(b, inner):
+                rows = pl.ds(pl.multiple_of(b * 256, 256), 256)
+                s = lax.dot_general(
+                    q_cat[r, rows, :], key_buf[...], (((1,), (1,)), ((), ())), preferred_element_type=f32
+                )
+                s = s * temper + bias
+                before = top[r, rows, :1]
+                peak = jnp.maximum(before, jnp.max(s, axis=1, keepdims=True))
+                p = jnp.exp2(s - peak).astype(bf16)
+                acc[r, rows, :] = acc[r, rows, :] * jnp.exp2(before - peak) + jnp.dot(
+                    p, val_buf[...], preferred_element_type=f32
+                )
+                top[r, rows, :] = jnp.broadcast_to(peak, (256, LANES))
+                return inner
+
+            return lax.fori_loop(0, 4, one_block, carry)
+
+        lax.fori_loop(0, 4, one_request, 0)
+
+    def light_request(r):
+        spacing = (row_i - col_i).astype(f32)
+        steps = lax.broadcasted_iota(jnp.int32, (LANES, 1), 0).astype(f32)
+
+        def one_head(h, total):
+            rate = rates[h]
+            rows, cols = rows_of(r), rows_of(h)
+            q, k, v = q_in[rows, cols], k_in[rows, cols], v_in[rows, cols]
+            state = st_recv[table[st_place_at + r * 8 + h]]
+            weights = jnp.where(spacing >= 0.0, jnp.exp(-rate * jnp.maximum(spacing, 0.0)), 0.0)
+            s = lax.dot_general(q, k, (((1,), (1,)), ((), ())), preferred_element_type=f32) * weights
+            inside = jnp.dot(s.astype(bf16), v, preferred_element_type=f32)
+            carried = jnp.dot(q, state, preferred_element_type=f32) * jnp.exp(-rate * (steps + 1.0))
+            out = inside + carried
+            mix[rows, cols] = out
+            trail = k.astype(f32) * jnp.exp(-rate * (LANES - 1.0 - steps))
+            high = trail.astype(bf16)
+            low = (trail - high.astype(f32)).astype(bf16)
+            across = (((0,), (0,)), ((), ()))
+            state_out[r * 8 + h] = (
+                state.astype(f32) * jnp.exp(jnp.full((1, 1), -LANES, f32) * rate)
+                + lax.dot_general(high, v, across, preferred_element_type=f32)
+                + lax.dot_general(low, v, across, preferred_element_type=f32)
+            )
+            return total + jnp.sum(out * out, axis=1, keepdims=True)
+
+        total = lax.fori_loop(0, 8, one_head, jnp.zeros((LANES, 1), f32))
+        sq_send[r] = jnp.broadcast_to(total, (LANES, LANES)).T[:8, :]
+
+    def step(t, carry):
+        wait_bytes(a_buf.at[t], a_recv.at[t])
+        slot = lax.rem(t, 2)
+
+        @pl.when(t >= 2)
+        def _():
+            wait_bytes(s_buf.at[slot, pl.ds(0, 15 * row_cap)], b_send.at[slot])
+            wait_bytes(s_buf.at[slot, pl.ds(0, row_cap)], keep_sems.at[slot])
+
+        a_cur[...] = a_buf[t]
+
+        def pack(i, inner):
+            for c in range(row_cap):
+                s_buf[slot, i * row_cap + c] = a_cur[table[pick_at + i * row_cap + c]]
+            return inner
+
+        lax.fori_loop(0, 16, pack, 0)
+        mine = pl.ds(pool * row_cap, row_cap)
+        for d in pools_to:
+            pltpu.make_async_remote_copy(
+                s_buf.at[slot, pl.ds(d * row_cap, row_cap)],
+                r_buf.at[t, mine],
+                b_send.at[slot],
+                b_recv.at[t],
+                device_id={"pool": d},
+                device_id_type=MESH,
+            ).start()
+        pltpu.make_async_copy(s_buf.at[slot, mine], r_buf.at[t, mine], keep_sems.at[slot]).start()
+
+        @pl.when(t == 2)
+        def _():
+            wait_bytes(st_recv, st_sems.at[1])
+
+        @pl.when((t >= 2) & (t < 6))
+        def _():
+            light_request(t - 2)
+
+        @pl.when(t == 6)
+        def _():
+            sq_recv[head] = sq_send[...]
+            for d in heads_to:
+                pltpu.make_async_remote_copy(
+                    sq_send,
+                    sq_recv.at[head],
+                    sq_sems.at[0],
+                    sq_sems.at[1],
+                    device_id={"head": d},
+                    device_id_type=MESH,
+                ).start()
+
+        @pl.when(t >= 2)
+        def _():
+            attend_chunk(t - 2)
+
+        return carry
+
+    lax.fori_loop(0, CHUNKS, step, 0)
+    for slot in range(2):
+        wait_bytes(s_buf.at[slot, pl.ds(0, 15 * row_cap)], b_send.at[slot])
+        wait_bytes(s_buf.at[slot, pl.ds(0, row_cap)], keep_sems.at[slot])
+    wait_bytes(sq_recv.at[pl.ds(0, 7)], sq_sems.at[1])
+
+    def finish_light(r, carry):
+        squares = jnp.sum(sq_recv[:, r, :1, :], axis=0)
+        factor = lax.rsqrt(squares / (64.0 * LANES) + 1e-06)
+        column = jnp.broadcast_to(factor, (LANES, LANES)).T[:, :1]
+        rows = rows_of(r)
+        gate = jax.nn.sigmoid(gate_in[rows, :].astype(f32))
+        light_out[rows, :] = (mix[rows, :] * column * gain_in[...] * gate).astype(bf16)
+        return carry
+
+    lax.fori_loop(0, 4, finish_light, 0)
+    attend_chunk(CHUNKS - 2)
+    attend_chunk(CHUNKS - 1)
+
+    def finish_soft(e, carry):
+        r, h = e // 8, lax.rem(e, 8)
+        soft_out[rows_of(r), rows_of(h)] = (
+            acc[r, rows_of(h), :LANES] / acc[r, rows_of(h), LANES:]
+        ).astype(bf16)
+        return carry
+
+    lax.fori_loop(0, 32, finish_soft, 0)
+
+    def drain(t, carry):
+        wait_bytes(a_buf.at[t, pl.ds(0, 112)], a_send.at[t])
+        return carry
+
+    lax.fori_loop(0, CHUNKS, drain, 0)
+    wait_bytes(st_send.at[pl.ds(0, 15 * STATE_CAP)], st_sems.at[0])
+    wait_bytes(sq_recv.at[pl.ds(0, 7)], sq_sems.at[0])
+
+
+def fused_call(row_cap, table, rates, q, k, v, gate, gain, store, soft_q, pair, kv):
+    tokens = LANES // CHUNKS
+    bf16, f32 = jnp.bfloat16, jnp.float32
+    vmem, smem = pl.BlockSpec(memory_space=pltpu.VMEM), pl.BlockSpec(memory_space=pltpu.SMEM)
+    dma = pltpu.SemaphoreType.DMA
+    return pl.pallas_call(
+        functools.partial(fused_kernel, row_cap),
+        out_shape=(
+            jax.ShapeDtypeStruct((512, 1024), bf16),
+            jax.ShapeDtypeStruct((32, LANES, LANES), f32),
+            jax.ShapeDtypeStruct((512, 1024), bf16),
+        ),
+        in_specs=[smem, smem] + [vmem] * 8 + [pl.BlockSpec(memory_space=pl.ANY)],
+        out_specs=(vmem, vmem, vmem),
+        scratch_shapes=[
+            pltpu.VMEM((CHUNKS, 128, tokens, 256), bf16),
+            pltpu.VMEM((128, tokens, 256), bf16),
+            pltpu.VMEM((2, 16 * row_cap, tokens, 256), bf16),
+            pltpu.VMEM((CHUNKS, 16 * row_cap, tokens, 256), bf16),
+            pltpu.VMEM((16 * row_cap, tokens, 256), bf16),
+            pltpu.VMEM((32 * tokens, LANES), bf16),
+            pltpu.VMEM((32 * tokens, 2 * LANES), bf16),
+            pltpu.VMEM((16 * STATE_CAP, LANES, LANES), bf16),
+            pltpu.VMEM((16 * STATE_CAP, LANES, LANES), bf16),
+            pltpu.VMEM((512, 1024), f32),
+            pltpu.VMEM((4, 8, LANES), f32),
+            pltpu.VMEM((8, 4, 8, LANES), f32),
+            pltpu.VMEM((4, 1024, LANES), bf16),
+            pltpu.VMEM((4, 1024, 2 * LANES), f32),
+            pltpu.VMEM((4, 1024, LANES), f32),
+            dma((CHUNKS,)),
+            dma((CHUNKS,)),
+            dma((2,)),
+            dma((CHUNKS,)),
+            dma((2,)),
+            dma((2,)),
+            dma((2,)),
+        ],
+        compiler_params=pltpu.CompilerParams(
+            collective_id=1, has_side_effects=True, vmem_limit_bytes=60 * 2**20
+        ),
+        cost_estimate=pl.CostEstimate(flops=10**10, bytes_accessed=3 * 10**7, transcendentals=2 * 10**7),
+    )(table, rates, q, k, v, gate, gain, store, soft_q, pair, kv)
+
+
+def exclusive_rank(match):
+    size = match.shape[-1]
+    order = jnp.arange(size)
+    before = (order[:, None] < order[None, :]).astype(jnp.bfloat16)
+    return jnp.dot(match.astype(jnp.bfloat16), before, preferred_element_type=jnp.float32).astype(jnp.int32)
+
+
+def pick_lists(match, values, capacity):
+    rank = exclusive_rank(match)
+    chosen = match[:, None, :] & (rank[:, None, :] == jnp.arange(capacity)[None, :, None])
+    return jnp.sum(jnp.where(chosen, values[:, None, :], 0), axis=2).reshape(-1)
+
+
+def own_places(rows, valid, capacity):
+    order = jnp.arange(rows.shape[0])
+    same = (rows[:, None] == rows[None, :]) & valid[None, :] & (order[None, :] < order[:, None])
+    return rows * capacity + jnp.sum(same.astype(jnp.int32), axis=1)
+
+
+def plan(state_slot, page_holder, page_local, prefix_len):
+    owner = lax.axis_index("pool")
+    pages = page_holder[:, :, 0] * 16 + page_local
+    active = jnp.arange(32)[None, :] * LANES < prefix_len[:, None]
+    own_pages = jnp.where(active, pages, 4095).reshape(-1)
+    own_states = state_slot.reshape(-1)
+    everyone = lax.all_gather(jnp.concatenate([own_pages, own_states]), "pool")
+    all_pages, all_states = everyone[:, :128], everyone[:, 128:]
+    page_rows = all_pages // 128
+    picks = pick_lists(page_rows == owner, all_pages % 128, ROW_CAP)
+    counts = jnp.sum((page_rows[:, :, None] == jnp.arange(16)[None, None, :]).astype(jnp.int32), axis=1)
+    fits = jnp.max(counts) <= ROW_CAP
+    places = own_places(own_pages // 128, active.reshape(-1), ROW_CAP).reshape(4, 32)
+    places = jnp.where(active, places, places[:, :1]).reshape(-1)
+    within = jnp.arange(32) % 8
+    state_picks = pick_lists(all_states // 4 == owner, all_states % 4 * 8 + within[None, :], STATE_CAP)
+    state_places = own_places(own_states // 4, jnp.ones((32,), bool), STATE_CAP)
+    table = jnp.concatenate([picks, places, prefix_len, state_picks, state_places]).astype(jnp.int32)
+    return table, fits
+
+
+def body(
+    light_query,
+    light_key,
+    light_value,
+    light_gate,
+    decay_rate,
+    norm_gain,
+    state_store,
+    state_slot,
+    soft_query,
+    soft_pair,
+    kv_store,
+    page_holder,
+    page_local,
+    prefix_len,
+):
+    table, fits = plan(state_slot, page_holder, page_local, prefix_len)
+
+    def quick():
+        light, states, soft = fused_call(
+            ROW_CAP,
+            table,
+            decay_rate,
+            light_query,
+            light_key,
+            light_value,
+            light_gate,
+            norm_gain.reshape(1, -1),
+            state_store.reshape(32, LANES, LANES),
+            soft_query,
+            soft_pair,
+            kv_store,
+        )
+        return light, states.reshape(4, 8, LANES, LANES), soft
+
+    def general():
+        return general_body(
+            light_query,
+            light_key,
+            light_value,
+            light_gate,
+            decay_rate,
+            norm_gain,
+            state_store,
+            state_slot,
+            soft_query,
+            soft_pair,
+            kv_store,
+            page_holder,
+            page_local,
+            prefix_len,
+        )
+
+    return lax.cond(fits, quick, general)
+
+
 def solution(mesh):
     return jax.shard_map(
         body,

time: 524 us -> 295 us (0.56)
  the two profiles are of different devices: /device:TPU:98 before, /device:TPU:1 now
where the time goes in v1:
time: 295 us; the launch traced here: 294 us
  Pallas kernels  217 us (74%)
  blocking collectives  62.4 us (21%)
  local copies, waits for them, and re-layouts  8.97 us (3%)
  other arithmetic  3.52 us (1%)
    pallas_call x1, Pallas kernels, fused_call(): pl.pallas_call(functools.partial(fused_kernel, row_cap), out_shape=(jax.S...  217 us
    unnamed x1, blocking collectives  62.4 us
    unnamed x9, local copies, waits for them, and re-layouts  6.58 us

profile of v1, /device:TPU:1, one launch (start us, length us, event | category | flops | bytes accessed | tf_op | source)
XLA Modules:
  0.0 294.3 jit_solution(11946564259266043742)
XLA Ops:
  0.6 0.7 broadcast_multiply_fusion.2
  1.3 0.8 add_select_fusion.7
  2.2 0.8 reshape.824
  2.9 1.2 dynamic-slice
  4.8 0.1 add_dynamic-update-slice_fusion
  5.0 62.4 %all-reduce = s32[2560]{0:T(1024)S(1)} all-reduce(s32[2560]{0:T(1024)S(1)} %add_dynamic-update-slice_fusion), channel_id=2, replica_groups=mesh['pool'=16,'head'=8] {'pool'}, use_global_device_ids=true, to_apply=%add | all-reduce | flops 2560 | bytes 20480
  67.4 0.1 convolution_convert_fusion.1
  67.6 0.3 select_reduce_fusion.2
  67.9 0.1 reshape.825
  68.1 0.1 convolution_convert_fusion
  68.2 0.1 select_reduce_fusion.3
  68.4 0.1 reshape.827
  68.6 0.2 convert_reduce_fusion.1
  68.9 0.1 slice_reduce_fusion
  69.2 0.2 convert_reduce_fusion.2
  69.4 0.7 concatenate.13
  70.2 0.3 convert_reduce_fusion
  70.5 0.6 reduce_max.22
  71.8 217.2 %conditional.1 = (bf16[512,1024]{1,0:T(8,128)(2,1)}, f32[4,8,128,128]{3,2,1,0:T(8,128)}, bf16[512,1024]{1,0:T(8,128)(2,1)}) conditional(s32[]{:T(128)} %convert_element_type.134, (bf16[512,1024]{1,0:T(8,128)(2,1)}, bf16[512,1024]{1,0:T(8,128)(2,1)}, f32[8]{0:T(128)}, bf16[512,1024]{1,0:T(8,128)(2,1)}, s32[4,8]{1,0:T(4,128)}, ...), branch_computations={%region_6.19_spmd, %region_19.20_spmd} | conditional | flops 10000000000 | bytes 313822720 | solution.py:629
  72.0 216.9 %branch_1_fun.1 = (bf16[512,1024]{1,0:T(8,128)(2,1)}, f32[32,128,128]{2,1,0:T(8,128)}, bf16[512,1024]{1,0:T(8,128)(2,1)}) custom-call(s32[404]{0:T(512)S(1)} %get-tuple-element.170.table, f32[8]{0:T(128)} %get-tuple-element.171.rates, bf16[512,1024]{1,0:T(8,128)(2,1)} %get-tuple-element.172.q_in, bf16[512,1024]{1,0:T(8,128)(2,1)} %get-tuple-element.173.k_in, ...), custom_call_target="tpu_custom_call" | custom-call | flops 10000000000 | bytes 30000000 | tf_op jit(solution)/shard_map/cond/branch_1_fun/pallas_call | solution.py:496
  289.0 2.4 copy.171
  291.4 1.3 copy.172
  292.7 0.6 copy-done.6
  293.4 1.0 copy.173
  (22 shorter events, 0.8 us)
Async XLA Ops:
  289.0 2.4 copy-start.2
  291.4 2.0 copy-start.6

commit v2 on v1

--- a/solution.py
+++ b/solution.py
@@ -215,10 +215,58 @@
     pltpu.make_async_copy(ref, ref, sem).wait()
 
 
+def make_lists(row_cap, pool, wants, asked, lists, crowd_out):
+    i32 = jnp.int32
+    lane = lax.broadcasted_iota(i32, (16, LANES), 1)
+    row = lax.broadcasted_iota(i32, (16, LANES), 0)
+    pages, states = asked[:, 0, :], asked[:, 1, :]
+    own_pages = jnp.broadcast_to(wants[0:1, :], (16, LANES))
+    own_states = jnp.broadcast_to(wants[1:2, :], (16, LANES))
+    page_match = (pages // 128 == pool).astype(i32)
+    state_match = (states // 4 == pool).astype(i32)
+    own_page_match = (own_pages // 128 == row).astype(i32)
+    own_state_match = (own_states // 4 == row).astype(i32)
+
+    def over_lanes(x):
+        for shift in (1, 2, 4, 8, 16, 32, 64):
+            x = x + pltpu.roll(x, shift, 1)
+        return x
+
+    def earlier(x):
+        total = x
+        for shift in (1, 2, 4, 8, 16, 32, 64):
+            total = total + jnp.where(lane >= shift, pltpu.roll(total, shift, 1), 0)
+        return total - x
+
+    def picks(match, values, capacity):
+        rank = earlier(match)
+        found = jnp.zeros((16, LANES), i32)
+        for c in range(capacity):
+            spot = over_lanes(jnp.where((match == 1) & (rank == c), values, 0))
+            found = jnp.where(lane == c, spot, found)
+        return found
+
+    def places(match, capacity):
+        spot = match * (row * capacity + jnp.minimum(earlier(match), capacity - 1))
+        return jnp.broadcast_to(jnp.sum(spot, axis=0, keepdims=True), (1, LANES))
+
+    lists[0:16, :] = picks(page_match, lax.rem(pages, 128), row_cap)
+    lists[16:32, :] = picks(state_match, lax.rem(states, 4) * 8 + lax.rem(lane, 8), STATE_CAP)
+    lists[32:33, :] = places(own_page_match, row_cap)
+    lists[33:34, :] = places(own_state_match, STATE_CAP)
+    lists[34:40, :] = jnp.zeros((6, LANES), i32)
+    most = jnp.zeros((16, 1), jnp.float32)
+    for j in range(16):
+        here = (pages // 128 == j).astype(jnp.float32)
+        most = jnp.maximum(most, jnp.sum(here, axis=1, keepdims=True))
+    crowd_out[...] = jnp.broadcast_to(jnp.max(most, axis=0, keepdims=True), (8, LANES))
+
+
 def fused_kernel(
     row_cap,
-    table,
+    lengths,
     rates,
+    wants,
     q_in,
     k_in,
     v_in,
@@ -231,6 +279,7 @@
     light_out,
     state_out,
     soft_out,
+    crowd_out,
     a_buf,
     a_cur,
     s_buf,
@@ -253,6 +302,11 @@
     keep_sems,
     st_sems,
     sq_sems,
+    asked,
+    lists,
+    table,
+    ask_sems,
+    list_sem,
 ):
     f32, bf16 = jnp.float32, jnp.bfloat16
     tokens = LANES // CHUNKS
@@ -262,8 +316,6 @@
     hy, hc = head // 2, lax.rem(head, 2)
     heads_to = [lax.rem(hy + k // 2, 4) * 2 + lax.rem(hc + k % 2, 2) for k in range(1, 8)]
     pools_to = [lax.rem(px + k // 4, 4) * 4 + lax.rem(pz + k % 4, 4) for k in range(1, 16)]
-    pick_at, place_at, len_at = 0, 16 * row_cap, 16 * row_cap + 128
-    st_pick_at, st_place_at = len_at + 4, len_at + 4 + 64
 
     barrier = pltpu.get_barrier_semaphore()
     for d in heads_to:
@@ -271,6 +323,17 @@
     for d in pools_to:
         pl.semaphore_signal(barrier, inc=1, device_id={"pool": d}, device_id_type=MESH)
     pl.semaphore_wait(barrier, 22)
+
+    for d in pools_to:
+        pltpu.make_async_remote_copy(
+            wants,
+            asked.at[pool],
+            ask_sems.at[0],
+            ask_sems.at[1],
+            device_id={"pool": d},
+            device_id_type=MESH,
+        ).start()
+    asked[pool] = wants[...]
 
     def send_store(t, carry):
         part = pl.ds(pl.multiple_of(t * tokens, tokens), tokens)
@@ -288,11 +351,17 @@
         ).start()
         return carry
 
-    lax.fori_loop(0, CHUNKS, send_store, 0)
+    lax.fori_loop(0, 2, send_store, 0)
+
+    wait_bytes(asked.at[pl.ds(0, 15)], ask_sems.at[1])
+    make_lists(row_cap, pool, wants, asked, lists, crowd_out)
+    to_scalars = pltpu.make_async_copy(lists, table, list_sem)
+    to_scalars.start()
+    to_scalars.wait()
 
     def pack_state(i, carry):
         for c in range(STATE_CAP):
-            st_send[i * STATE_CAP + c] = store_in[table[st_pick_at + i * STATE_CAP + c]].astype(bf16)
+            st_send[i * STATE_CAP + c] = store_in[table[16 + i, c]].astype(bf16)
         return carry
 
     lax.fori_loop(0, 16, pack_state, 0)
@@ -308,8 +377,9 @@
         ).start()
     pltpu.make_async_copy(st_send.at[mine_st], st_recv.at[mine_st], st_sems.at[1]).start()
 
+    lax.fori_loop(2, CHUNKS, send_store, 0)
+
     temper = LOG2E / math.sqrt(LANES)
-    val_buf[:, LANES:] = jnp.ones((keys, LANES), bf16)
     row_i = lax.broadcasted_iota(jnp.int32, (LANES, LANES), 0)
     col_i = lax.broadcasted_iota(jnp.int32, (LANES, LANES), 1)
 
@@ -325,9 +395,9 @@
         s = lax.dot_general(q, k, (((1,), (1,)), ((), ())), preferred_element_type=f32) * temper
         s = jnp.where(col_i <= row_i, s, -1e30)
         peak = jnp.max(s, axis=1, keepdims=True)
-        p = jnp.exp2(s - peak).astype(bf16)
-        acc[r, rows_of(h), :LANES] = jnp.dot(p, v, preferred_element_type=f32)
-        acc[r, rows_of(h), LANES:] = jnp.dot(p, jnp.ones((LANES, LANES), bf16), preferred_element_type=f32)
+        p = jnp.exp2(s - peak)
+        acc[r, rows_of(h), :LANES] = jnp.dot(p.astype(bf16), v, preferred_element_type=f32)
+        acc[r, rows_of(h), LANES:] = p
         top[r, rows_of(h), :] = jnp.broadcast_to(peak, (LANES, LANES))
         return carry
 
@@ -337,32 +407,34 @@
 
     def attend_chunk(t):
         wait_bytes(r_buf.at[t, pl.ds(0, 15 * row_cap)], b_recv.at[t])
+        wait_bytes(r_buf.at[t, pl.ds(0, row_cap)], keep_sems.at[lax.rem(t, 2)])
         r_cur[...] = r_buf[t]
         spot = (lane // tokens) * LANES + t * tokens + lax.rem(lane, tokens)
 
         def one_request(r, carry):
             for p in range(32):
-                block = r_cur[table[place_at + r * 32 + p]]
+                block = r_cur[table[32, r * 32 + p]]
                 key_buf[p * tokens : (p + 1) * tokens, :] = block[:, :LANES]
-                val_buf[p * tokens : (p + 1) * tokens, :LANES] = block[:, LANES:]
-            bias = jnp.where(spot < table[len_at + r], 0.0, -1e30).astype(f32)
-
-            def one_block(b, inner):
-                rows = pl.ds(pl.multiple_of(b * 256, 256), 256)
-                s = lax.dot_general(
-                    q_cat[r, rows, :], key_buf[...], (((1,), (1,)), ((), ())), preferred_element_type=f32
-                )
-                s = s * temper + bias
-                before = top[r, rows, :1]
-                peak = jnp.maximum(before, jnp.max(s, axis=1, keepdims=True))
-                p = jnp.exp2(s - peak).astype(bf16)
-                acc[r, rows, :] = acc[r, rows, :] * jnp.exp2(before - peak) + jnp.dot(
-                    p, val_buf[...], preferred_element_type=f32
-                )
-                top[r, rows, :] = jnp.broadcast_to(peak, (256, LANES))
-                return inner
-
-            return lax.fori_loop(0, 4, one_block, carry)
+                val_buf[p * tokens : (p + 1) * tokens, :] = block[:, LANES:]
+            bias = jnp.where(spot < lengths[r], 0.0, -1e30).astype(f32)
+
+            s = lax.dot_general(
+                q_cat[r], key_buf[...], (((1,), (1,)), ((), ())), preferred_element_type=f32
+            )
+            s = s * temper + bias
+            before = top[r]
+            peak = jnp.maximum(before, jnp.max(s, axis=1, keepdims=True))
+            p = jnp.exp2(s - jnp.concatenate([peak] * (keys // LANES), axis=1))
+            shrink = jnp.exp2(before - peak)
+            acc[r, :, :LANES] = acc[r, :, :LANES] * shrink + jnp.dot(
+                p.astype(bf16), val_buf[...], preferred_element_type=f32
+            )
+            sums = p[:, :LANES]
+            for part in range(1, keys // LANES):
+                sums = sums + p[:, part * LANES : (part + 1) * LANES]
+            acc[r, :, LANES:] = acc[r, :, LANES:] * shrink + sums
+            top[r] = peak
+            return carry
 
         lax.fori_loop(0, 4, one_request, 0)
 
@@ -374,7 +446,7 @@
             rate = rates[h]
             rows, cols = rows_of(r), rows_of(h)
             q, k, v = q_in[rows, cols], k_in[rows, cols], v_in[rows, cols]
-            state = st_recv[table[st_place_at + r * 8 + h]]
+            state = st_recv[table[33, r * 8 + h]]
             weights = jnp.where(spacing >= 0.0, jnp.exp(-rate * jnp.maximum(spacing, 0.0)), 0.0)
             s = lax.dot_general(q, k, (((1,), (1,)), ((), ())), preferred_element_type=f32) * weights
             inside = jnp.dot(s.astype(bf16), v, preferred_element_type=f32)
@@ -402,13 +474,12 @@
         @pl.when(t >= 2)
         def _():
             wait_bytes(s_buf.at[slot, pl.ds(0, 15 * row_cap)], b_send.at[slot])
-            wait_bytes(s_buf.at[slot, pl.ds(0, row_cap)], keep_sems.at[slot])
 
         a_cur[...] = a_buf[t]
 
         def pack(i, inner):
             for c in range(row_cap):
-                s_buf[slot, i * row_cap + c] = a_cur[table[pick_at + i * row_cap + c]]
+                s_buf[slot, i * row_cap + c] = a_cur[table[i, c]]
             return inner
 
         lax.fori_loop(0, 16, pack, 0)
@@ -445,16 +516,15 @@
                     device_id_type=MESH,
                 ).start()
 
-        @pl.when(t >= 2)
+        @pl.when(t >= 1)
         def _():
-            attend_chunk(t - 2)
+            attend_chunk(t - 1)
 
         return carry
 
     lax.fori_loop(0, CHUNKS, step, 0)
     for slot in range(2):
         wait_bytes(s_buf.at[slot, pl.ds(0, 15 * row_cap)], b_send.at[slot])
-        wait_bytes(s_buf.at[slot, pl.ds(0, row_cap)], keep_sems.at[slot])
     wait_bytes(sq_recv.at[pl.ds(0, 7)], sq_sems.at[1])
 
     def finish_light(r, carry):
@@ -467,13 +537,12 @@
         return carry
 
     lax.fori_loop(0, 4, finish_light, 0)
-    attend_chunk(CHUNKS - 2)
-    attend_chunk(CHUNKS - 1)
+    attend_chunk(jnp.int32(CHUNKS - 1))
 
     def finish_soft(e, carry):
         r, h = e // 8, lax.rem(e, 8)
         soft_out[rows_of(r), rows_of(h)] = (
-            acc[r, rows_of(h), :LANES] / acc[r, rows_of(h), LANES:]
+            acc[r, rows_of(h), :LANES] / jnp.sum(acc[r, rows_of(h), LANES:], axis=1, keepdims=True)
         ).astype(bf16)
         return carry
 
@@ -486,9 +555,10 @@
     lax.fori_loop(0, CHUNKS, drain, 0)
     wait_bytes(st_send.at[pl.ds(0, 15 * STATE_CAP)], st_sems.at[0])
     wait_bytes(sq_recv.at[pl.ds(0, 7)], sq_sems.at[0])
-
-
-def fused_call(row_cap, table, rates, q, k, v, gate, gain, store, soft_q, pair, kv):
+    wait_bytes(asked.at[pl.ds(0, 15)], ask_sems.at[0])
+
+
+def fused_call(row_cap, lengths, rates, wants, q, k, v, gate, gain, store, soft_q, pair, kv):
     tokens = LANES // CHUNKS
     bf16, f32 = jnp.bfloat16, jnp.float32
     vmem, smem = pl.BlockSpec(memory_space=pltpu.VMEM), pl.BlockSpec(memory_space=pltpu.SMEM)
@@ -499,9 +569,10 @@
             jax.ShapeDtypeStruct((512, 1024), bf16),
             jax.ShapeDtypeStruct((32, LANES, LANES), f32),
             jax.ShapeDtypeStruct((512, 1024), bf16),
+            jax.ShapeDtypeStruct((8, LANES), f32),
         ),
-        in_specs=[smem, smem] + [vmem] * 8 + [pl.BlockSpec(memory_space=pl.ANY)],
-        out_specs=(vmem, vmem, vmem),
+        in_specs=[smem, smem] + [vmem] * 9 + [pl.BlockSpec(memory_space=pl.ANY)],
+        out_specs=(vmem, vmem, vmem, vmem),
         scratch_shapes=[
             pltpu.VMEM((CHUNKS, 128, tokens, 256), bf16),
             pltpu.VMEM((128, tokens, 256), bf16),
@@ -509,7 +580,7 @@
             pltpu.VMEM((CHUNKS, 16 * row_cap, tokens, 256), bf16),
             pltpu.VMEM((16 * row_cap, tokens, 256), bf16),
             pltpu.VMEM((32 * tokens, LANES), bf16),
-            pltpu.VMEM((32 * tokens, 2 * LANES), bf16),
+            pltpu.VMEM((32 * tokens, LANES), bf16),
             pltpu.VMEM((16 * STATE_CAP, LANES, LANES), bf16),
             pltpu.VMEM((16 * STATE_CAP, LANES, LANES), bf16),
             pltpu.VMEM((512, 1024), f32),
@@ -525,52 +596,25 @@
             dma((2,)),
             dma((2,)),
             dma((2,)),
+            pltpu.VMEM((16, 8, LANES), jnp.int32),
+            pltpu.VMEM((40, LANES), jnp.int32),
+            pltpu.SMEM((40, LANES), jnp.int32),
+            dma((2,)),
+            dma,
         ],
         compiler_params=pltpu.CompilerParams(
             collective_id=1, has_side_effects=True, vmem_limit_bytes=60 * 2**20
         ),
         cost_estimate=pl.CostEstimate(flops=10**10, bytes_accessed=3 * 10**7, transcendentals=2 * 10**7),
-    )(table, rates, q, k, v, gate, gain, store, soft_q, pair, kv)
-
-
-def exclusive_rank(match):
-    size = match.shape[-1]
-    order = jnp.arange(size)
-    before = (order[:, None] < order[None, :]).astype(jnp.bfloat16)
-    return jnp.dot(match.astype(jnp.bfloat16), before, preferred_element_type=jnp.float32).astype(jnp.int32)
-
-
-def pick_lists(match, values, capacity):
-    rank = exclusive_rank(match)
-    chosen = match[:, None, :] & (rank[:, None, :] == jnp.arange(capacity)[None, :, None])
-    return jnp.sum(jnp.where(chosen, values[:, None, :], 0), axis=2).reshape(-1)
-
-
-def own_places(rows, valid, capacity):
-    order = jnp.arange(rows.shape[0])
-    same = (rows[:, None] == rows[None, :]) & valid[None, :] & (order[None, :] < order[:, None])
-    return rows * capacity + jnp.sum(same.astype(jnp.int32), axis=1)
-
-
-def plan(state_slot, page_holder, page_local, prefix_len):
-    owner = lax.axis_index("pool")
+    )(lengths, rates, wants, q, k, v, gate, gain, store, soft_q, pair, kv)
+
+
+def wanted(state_slot, page_holder, page_local, prefix_len):
     pages = page_holder[:, :, 0] * 16 + page_local
     active = jnp.arange(32)[None, :] * LANES < prefix_len[:, None]
-    own_pages = jnp.where(active, pages, 4095).reshape(-1)
-    own_states = state_slot.reshape(-1)
-    everyone = lax.all_gather(jnp.concatenate([own_pages, own_states]), "pool")
-    all_pages, all_states = everyone[:, :128], everyone[:, 128:]
-    page_rows = all_pages // 128
-    picks = pick_lists(page_rows == owner, all_pages % 128, ROW_CAP)
-    counts = jnp.sum((page_rows[:, :, None] == jnp.arange(16)[None, None, :]).astype(jnp.int32), axis=1)
-    fits = jnp.max(counts) <= ROW_CAP
-    places = own_places(own_pages // 128, active.reshape(-1), ROW_CAP).reshape(4, 32)
-    places = jnp.where(active, places, places[:, :1]).reshape(-1)
-    within = jnp.arange(32) % 8
-    state_picks = pick_lists(all_states // 4 == owner, all_states % 4 * 8 + within[None, :], STATE_CAP)
-    state_places = own_places(own_states // 4, jnp.ones((32,), bool), STATE_CAP)
-    table = jnp.concatenate([picks, places, prefix_len, state_picks, state_places]).astype(jnp.int32)
-    return table, fits
+    own_pages = jnp.where(active, pages, 4095).reshape(1, -1)
+    own_states = jnp.pad(state_slot.reshape(1, -1), ((0, 0), (0, 96)), constant_values=255)
+    return jnp.concatenate([own_pages, own_states, jnp.zeros((6, LANES), jnp.int32)]).astype(jnp.int32)
 
 
 def body(
@@ -589,23 +633,23 @@
     page_local,
     prefix_len,
 ):
-    table, fits = plan(state_slot, page_holder, page_local, prefix_len)
+    light, states, soft, crowd = fused_call(
+        ROW_CAP,
+        prefix_len,
+        decay_rate,
+        wanted(state_slot, page_holder, page_local, prefix_len),
+        light_query,
+        light_key,
+        light_value,
+        light_gate,
+        norm_gain.reshape(1, -1),
+        state_store.reshape(32, LANES, LANES),
+        soft_query,
+        soft_pair,
+        kv_store,
+    )
 
     def quick():
-        light, states, soft = fused_call(
-            ROW_CAP,
-            table,
-            decay_rate,
-            light_query,
-            light_key,
-            light_value,
-            light_gate,
-            norm_gain.reshape(1, -1),
-            state_store.reshape(32, LANES, LANES),
-            soft_query,
-            soft_pair,
-            kv_store,
-        )
         return light, states.reshape(4, 8, LANES, LANES), soft
 
     def general():
@@ -626,7 +670,7 @@
             prefix_len,
         )
 
-    return lax.cond(fits, quick, general)
+    return lax.cond(crowd[0, 0] <= ROW_CAP, quick, general)
 
 
 def solution(mesh):

time: 295 us -> 199 us (0.67)
  blocking collectives: 62.4 us -> 0 us
  Pallas kernels: 217 us -> 187 us
    unnamed x1 -> x0, blocking collectives: 62.4 us -> none
    pallas_call x1, Pallas kernels: 217 us -> 187 us  [fused_call(): pl.pallas_call(functools.partial(fused_kernel, row_cap), out_shape=(jax.S...]
    unnamed x9 -> x21, local copies, waits for them, and re-layouts: 6.58 us -> 5.38 us
where the time goes in v2:
time: 199 us; the launch traced here: 198 us
  Pallas kernels  187 us (94%)
  local copies, waits for them, and re-layouts  7.5 us (4%)
  other arithmetic  2.11 us (1%)
    pallas_call x1, Pallas kernels, fused_call(): pl.pallas_call(functools.partial(fused_kernel, row_cap), out_shape=(jax.S...  187 us
    unnamed x21, local copies, waits for them, and re-layouts  5.38 us

profile of v2, /device:TPU:1, one launch (start us, length us, event | category | flops | bytes accessed | tf_op | source)
XLA Modules:
  0.0 197.9 jit_solution(12171554751759191043)
XLA Ops:
  0.6 0.7 broadcast_multiply_fusion.2
  1.3 0.8 add_select_fusion.2
  2.1 0.1 reshape.674
  2.2 0.1 pad.9.clone
  2.2 0.8 reshape.675
  3.0 0.7 fusion.59.wants
  3.7 0.0 copy-start.10
  3.7 0.0 copy-start.11
  3.7 0.0 copy-start.13
  3.7 186.6 %shard_map.163 = (bf16[512,1024]{1,0:T(8,128)(2,1)}, f32[32,128,128]{2,1,0:T(8,128)}, bf16[512,1024]{1,0:T(8,128)(2,1)}, f32[8,128]{1,0:T(8,128)}) custom-call(s32[4]{0:T(128)} %lengths.1, f32[8]{0:T(128)} %rates.1, s32[8,128]{1,0:T(8,128)} %fusion.59.wants, bf16[512,1024]{1,0:T(8,128)(2,1)} %q_in.1, bf16[512,1024]{1,0:T(8,128)(2,1)} %k_in.1, ...), custom_call_target="tpu_custom_call" | custom-call | flops 10000000000 | bytes 30000000 | tf_op jit(solution)/shard_map/pallas_call | solution.py:566
  190.4 1.2 slice.17
  192.2 0.0 copy-done.2
  192.2 0.0 copy-done.6
  192.2 0.0 copy-done.8
  192.2 0.0 copy-done.9
  192.2 0.0 copy-done.10
  192.3 0.0 copy-done.11
  192.3 0.0 copy-done.13
  192.3 0.2 conditional.1
  192.5 0.0 copy-start.4
  192.5 2.4 %copy.149 = bf16[512,1024]{1,0:T(8,128)(2,1)} copy(bf16[512,1024]{1,0:T(8,128)(2,1)} %get-tuple-element.384) | data formatting | bytes 2097152
  194.9 1.3 copy.150
  196.3 0.6 copy-done.7
  196.9 1.0 copy.151
  (8 shorter events, 0.0 us)
Async XLA Ops:
  3.7 188.5 %copy-start.2 = (f32[4,8,128,128]{3,2,1,0:T(8,128)S(1)}, f32[4,8,128,128]{3,2,1,0:T(8,128)}, u32[]{:S(2)}) copy-start(f32[4,8,128,128]{3,2,1,0:T(8,128)} %param.24) | copy-start | bytes 6291460
  3.7 188.5 %copy-start.6 = (bf16[512,1024]{1,0:T(8,128)(2,1)S(1)}, bf16[512,1024]{1,0:T(8,128)(2,1)}, u32[]{:S(2)}) copy-start(bf16[512,1024]{1,0:T(8,128)(2,1)} %k_in.1) | copy-start | bytes 3145732
  3.7 188.6 %copy-start.8 = (s32[4,8]{1,0:T(4,128)S(1)}, s32[4,8]{1,0:T(4,128)}, u32[]{:S(2)}) copy-start(s32[4,8]{1,0:T(4,128)} %param.25) | copy-start | bytes 388
  3.7 188.6 %copy-start.9 = (s32[4,32,1]{1,2,0:T(1,128)S(1)}, s32[4,32,1]{1,2,0:T(1,128)}, u32[]{:S(2)}) copy-start(s32[4,32,1]{1,2,0:T(1,128)} %param.29) | copy-start | bytes 1540
  3.7 188.6 %copy-start.10 = (s32[4,32]{1,0:T(4,128)S(1)}, s32[4,32]{1,0:T(4,128)}, u32[]{:S(2)}) copy-start(s32[4,32]{1,0:T(4,128)} %param.30) | copy-start | bytes 1540
  3.7 188.6 %copy-start.11 = (f32[1024]{0:T(1024)S(1)}, f32[1024]{0:T(1024)}, u32[]{:S(2)}) copy-start(f32[1024]{0:T(1024)} %param.23) | copy-start | bytes 12292
  3.7 188.6 %copy-start.13 = (f32[8]{0:T(128)S(1)}, f32[8]{0:T(128)}, u32[]{:S(2)}) copy-start(f32[8]{0:T(128)} %rates.1) | copy-start | bytes 100
  192.5 2.4 %copy-start.4 = (f32[4,8,128,128]{3,2,1,0:T(8,128)S(1)}, f32[4,8,128,128]{3,2,1,0:T(8,128)}, u32[]{:S(2)}) copy-start(f32[4,8,128,128]{3,2,1,0:T(8,128)} %get-tuple-element.385) | copy-start | bytes 6291460
  194.9 2.0 copy-start.7

commit v3 on v2

--- a/solution.py
+++ b/solution.py
@@ -206,8 +206,10 @@
 MESH = pl.DeviceIdType.MESH
 LANES = 128
 CHUNKS = 8
-ROW_CAP = 11
+ROW_CAP = 8
+EXTRA = 6
 STATE_CAP = 4
+PIECE = 4
 LOG2E = 1.4426950408889634
 
 
@@ -215,51 +217,95 @@
     pltpu.make_async_copy(ref, ref, sem).wait()
 
 
-def make_lists(row_cap, pool, wants, asked, lists, crowd_out):
+def over_lanes(x):
+    for shift in (1, 2, 4, 8, 16, 32, 64):
+        x = x + pltpu.roll(x, shift, 1)
+    return x
+
+
+def earlier(x):
+    lane = lax.broadcasted_iota(jnp.int32, x.shape, 1)
+    total = x
+    for shift in (1, 2, 4, 8, 16, 32, 64):
+        total = total + jnp.where(lane >= shift, pltpu.roll(total, shift, 1), 0)
+    return total - x
+
+
+def picks(match, rank, values, capacity):
+    lane = lax.broadcasted_iota(jnp.int32, match.shape, 1)
+    found = jnp.zeros(match.shape, jnp.int32)
+    for c in range(capacity):
+        spot = over_lanes(jnp.where((match == 1) & (rank == c), values, 0))
+        found = jnp.where(lane == c, spot, found)
+    return found
+
+
+def state_lists(pool, wants, asked, lists):
+    lane = lax.broadcasted_iota(jnp.int32, (16, LANES), 1)
+    row = lax.broadcasted_iota(jnp.int32, (16, LANES), 0)
+    states = asked[:, 1, :]
+    match = (states // 4 == pool).astype(jnp.int32)
+    lists[0:16, :] = picks(match, earlier(match), lax.rem(states, 4) * 8 + lax.rem(lane, 8), STATE_CAP)
+    own = (jnp.broadcast_to(wants[1:2, :], (16, LANES)) // 4 == row).astype(jnp.int32)
+    spot = own * (row * STATE_CAP + jnp.minimum(earlier(own), STATE_CAP - 1))
+    lists[16:24, :] = jnp.broadcast_to(jnp.sum(spot, axis=0, keepdims=True), (8, LANES))
+
+
+def page_lists(row_cap, pool, wants, asked, lists):
     i32 = jnp.int32
     lane = lax.broadcasted_iota(i32, (16, LANES), 1)
     row = lax.broadcasted_iota(i32, (16, LANES), 0)
-    pages, states = asked[:, 0, :], asked[:, 1, :]
-    own_pages = jnp.broadcast_to(wants[0:1, :], (16, LANES))
-    own_states = jnp.broadcast_to(wants[1:2, :], (16, LANES))
-    page_match = (pages // 128 == pool).astype(i32)
-    state_match = (states // 4 == pool).astype(i32)
-    own_page_match = (own_pages // 128 == row).astype(i32)
-    own_state_match = (own_states // 4 == row).astype(i32)
-
-    def over_lanes(x):
-        for shift in (1, 2, 4, 8, 16, 32, 64):
-            x = x + pltpu.roll(x, shift, 1)
-        return x
-
-    def earlier(x):
-        total = x
-        for shift in (1, 2, 4, 8, 16, 32, 64):
-            total = total + jnp.where(lane >= shift, pltpu.roll(total, shift, 1), 0)
-        return total - x
-
-    def picks(match, values, capacity):
-        rank = earlier(match)
-        found = jnp.zeros((16, LANES), i32)
-        for c in range(capacity):
-            spot = over_lanes(jnp.where((match == 1) & (rank == c), values, 0))
-            found = jnp.where(lane == c, spot, found)
-        return found
-
-    def places(match, capacity):
-        spot = match * (row * capacity + jnp.minimum(earlier(match), capacity - 1))
-        return jnp.broadcast_to(jnp.sum(spot, axis=0, keepdims=True), (1, LANES))
-
-    lists[0:16, :] = picks(page_match, lax.rem(pages, 128), row_cap)
-    lists[16:32, :] = picks(state_match, lax.rem(states, 4) * 8 + lax.rem(lane, 8), STATE_CAP)
-    lists[32:33, :] = places(own_page_match, row_cap)
-    lists[33:34, :] = places(own_state_match, STATE_CAP)
-    lists[34:40, :] = jnp.zeros((6, LANES), i32)
-    most = jnp.zeros((16, 1), jnp.float32)
-    for j in range(16):
-        here = (pages // 128 == j).astype(jnp.float32)
-        most = jnp.maximum(most, jnp.sum(here, axis=1, keepdims=True))
-    crowd_out[...] = jnp.broadcast_to(jnp.max(most, axis=0, keepdims=True), (8, LANES))
+    row_x, row_z = row // 4, lax.rem(row, 4)
+    pool_z = lax.rem(pool, 4)
+    pages = asked[:, 0, :]
+    page_rows = pages // 128
+
+    def past(match):
+        return jnp.maximum(over_lanes(match) - row_cap, 0)
+
+    def before_z(x):
+        return sum(jnp.where(row_z >= k, pltpu.roll(x, k, 0), 0) for k in (1, 2, 3))
+
+    def before_x(x):
+        return sum(jnp.where(row_x >= k, pltpu.roll(x, 4 * k, 0), 0) for k in (1, 2, 3))
+
+    match = (page_rows == pool).astype(i32)
+    rank = earlier(match)
+    slots = lax.rem(pages, 128)
+    lists[0:16, :] = picks(match, rank, slots, row_cap)
+    spare = jnp.where(rank >= row_cap, before_z(past(match)) + rank - row_cap, -1)
+    lists[16:32, :] = picks(match, spare, slots, EXTRA)
+
+    relay = jnp.zeros((16, LANES), i32)
+    start = jnp.zeros((16, LANES), i32)
+    for x in range(4):
+        extra = past((page_rows == x * 4 + pool_z).astype(i32))
+        inside = (lane >= start) & (lane < start + extra)
+        at = jnp.minimum(before_z(extra) + lane - start, EXTRA - 1)
+        relay = jnp.where(inside, x * EXTRA + at, relay)
+        start = start + extra
+    lists[32:48, :] = relay
+
+    own = (jnp.broadcast_to(wants[0:1, :], (16, LANES)) // 128 == row).astype(i32)
+    own_rank = earlier(own)
+    beyond = jnp.clip(before_x(past(own)) + own_rank - row_cap, 0, EXTRA - 1)
+    spot = own * jnp.where(
+        own_rank < row_cap, row * row_cap + own_rank, 16 * row_cap + row_z * EXTRA + beyond
+    )
+
+    worst = jnp.zeros((16, LANES), i32)
+    for z in range(4):
+        along = jnp.zeros((16, LANES), i32)
+        for x in range(4):
+            extra = past((page_rows == x * 4 + z).astype(i32))
+            along = along + extra
+            worst = jnp.maximum(worst, before_z(extra) + extra)
+        worst = jnp.maximum(worst, along)
+    for shift in (1, 2, 4, 8):
+        worst = jnp.maximum(worst, pltpu.roll(worst, shift, 0))
+    lists[48:49, :] = jnp.broadcast_to(jnp.sum(spot, axis=0, keepdims=True), (1, LANES))
+    lists[49:50, :] = worst[0:1, :]
+    lists[50:56, :] = jnp.zeros((6, LANES), i32)
 
 
 def fused_kernel(
@@ -267,19 +313,26 @@
     lengths,
     rates,
     wants,
+    gain_in,
+    q_hbm,
+    k_hbm,
+    v_hbm,
+    gate_hbm,
+    store_hbm,
+    soft_q_hbm,
+    pair_hbm,
+    kv_ref,
+    light_hbm,
+    state_hbm,
+    soft_out,
+    crowd_out,
     q_in,
     k_in,
     v_in,
     gate_in,
-    gain_in,
-    store_in,
-    soft_q,
     pair_in,
-    kv_ref,
     light_out,
     state_out,
-    soft_out,
-    crowd_out,
     a_buf,
     a_cur,
     s_buf,
@@ -300,13 +353,25 @@
     b_send,
     b_recv,
     keep_sems,
+    xs_buf,
+    xo_buf,
+    xo_cur,
+    zs_buf,
+    x_send,
+    x_recv,
+    z_send,
+    z_recv,
     st_sems,
     sq_sems,
     asked,
+    st_lists,
+    st_table,
     lists,
     table,
     ask_sems,
-    list_sem,
+    list_sems,
+    in_sems,
+    out_sems,
 ):
     f32, bf16 = jnp.float32, jnp.bfloat16
     tokens = LANES // CHUNKS
@@ -315,7 +380,29 @@
     px, pz = pool // 4, lax.rem(pool, 4)
     hy, hc = head // 2, lax.rem(head, 2)
     heads_to = [lax.rem(hy + k // 2, 4) * 2 + lax.rem(hc + k % 2, 2) for k in range(1, 8)]
+    xs_to = [lax.rem(px + k, 4) for k in range(1, 4)]
+    zs_to = [lax.rem(pz + k, 4) for k in range(1, 4)]
     pools_to = [lax.rem(px + k // 4, 4) * 4 + lax.rem(pz + k % 4, 4) for k in range(1, 16)]
+
+    def rows_of(r):
+        return pl.ds(pl.multiple_of(r * LANES, LANES), LANES)
+
+    load_store = pltpu.make_async_copy(store_hbm, mix, in_sems.at[0])
+    load_pair = pltpu.make_async_copy(pair_hbm, pair_in, in_sems.at[1])
+    loads = [
+        pltpu.make_async_copy(source, target, in_sems.at[2 + n])
+        for n, (source, target) in enumerate(
+            ((q_hbm, q_in), (k_hbm, k_in), (v_hbm, v_in), (gate_hbm, gate_in))
+        )
+    ]
+    load_store.start()
+
+    def load_query(e, carry):
+        r, h = e // 8, lax.rem(e, 8)
+        pltpu.make_async_copy(
+            soft_q_hbm.at[rows_of(r), rows_of(h)], q_cat.at[r, rows_of(h)], in_sems.at[6]
+        ).start()
+        return carry
 
     barrier = pltpu.get_barrier_semaphore()
     for d in heads_to:
@@ -353,15 +440,21 @@
 
     lax.fori_loop(0, 2, send_store, 0)
 
+    load_pair.start()
+    lax.fori_loop(0, 32, load_query, 0)
+    for load in loads:
+        load.start()
     wait_bytes(asked.at[pl.ds(0, 15)], ask_sems.at[1])
-    make_lists(row_cap, pool, wants, asked, lists, crowd_out)
-    to_scalars = pltpu.make_async_copy(lists, table, list_sem)
+    state_lists(pool, wants, asked, st_lists)
+    to_scalars = pltpu.make_async_copy(st_lists, st_table, list_sems.at[0])
     to_scalars.start()
     to_scalars.wait()
 
+    load_store.wait()
+
     def pack_state(i, carry):
         for c in range(STATE_CAP):
-            st_send[i * STATE_CAP + c] = store_in[table[16 + i, c]].astype(bf16)
+            st_send[i * STATE_CAP + c] = mix[st_table[i, c]].astype(bf16)
         return carry
 
     lax.fori_loop(0, 16, pack_state, 0)
@@ -379,17 +472,19 @@
 
     lax.fori_loop(2, CHUNKS, send_store, 0)
 
+    page_lists(row_cap, pool, wants, asked, lists)
+    to_table = pltpu.make_async_copy(lists, table, list_sems.at[1])
+    to_table.start()
+    to_table.wait()
+    crowd_out[0, 0] = table[49, 0]
+
     temper = LOG2E / math.sqrt(LANES)
     row_i = lax.broadcasted_iota(jnp.int32, (LANES, LANES), 0)
     col_i = lax.broadcasted_iota(jnp.int32, (LANES, LANES), 1)
 
-    def rows_of(r):
-        return pl.ds(pl.multiple_of(r * LANES, LANES), LANES)
-
     def open_softmax(e, carry):
         r, h = e // 8, lax.rem(e, 8)
-        q = soft_q[rows_of(r), rows_of(h)]
-        q_cat[r, rows_of(h), :] = q
+        q = q_cat[r, rows_of(h), :]
         k = pair_in[rows_of(r), :LANES]
         v = pair_in[rows_of(r), LANES:]
         s = lax.dot_general(q, k, (((1,), (1,)), ((), ())), preferred_element_type=f32) * temper
@@ -401,6 +496,8 @@
         top[r, rows_of(h), :] = jnp.broadcast_to(peak, (LANES, LANES))
         return carry
 
+    load_pair.wait()
+    wait_bytes(q_cat, in_sems.at[6])
     lax.fori_loop(0, 32, open_softmax, 0)
 
     lane = lax.broadcasted_iota(jnp.int32, (1, keys), 1)
@@ -408,12 +505,13 @@
     def attend_chunk(t):
         wait_bytes(r_buf.at[t, pl.ds(0, 15 * row_cap)], b_recv.at[t])
         wait_bytes(r_buf.at[t, pl.ds(0, row_cap)], keep_sems.at[lax.rem(t, 2)])
+        wait_bytes(r_buf.at[t, pl.ds(0, 3 * EXTRA)], z_recv.at[t])
         r_cur[...] = r_buf[t]
         spot = (lane // tokens) * LANES + t * tokens + lax.rem(lane, tokens)
 
         def one_request(r, carry):
             for p in range(32):
-                block = r_cur[table[32, r * 32 + p]]
+                block = r_cur[table[48, r * 32 + p]]
                 key_buf[p * tokens : (p + 1) * tokens, :] = block[:, :LANES]
                 val_buf[p * tokens : (p + 1) * tokens, :] = block[:, LANES:]
             bias = jnp.where(spot < lengths[r], 0.0, -1e30).astype(f32)
@@ -446,13 +544,13 @@
             rate = rates[h]
             rows, cols = rows_of(r), rows_of(h)
             q, k, v = q_in[rows, cols], k_in[rows, cols], v_in[rows, cols]
-            state = st_recv[table[33, r * 8 + h]]
+            state = st_recv[st_table[16, r * 8 + h]]
             weights = jnp.where(spacing >= 0.0, jnp.exp(-rate * jnp.maximum(spacing, 0.0)), 0.0)
             s = lax.dot_general(q, k, (((1,), (1,)), ((), ())), preferred_element_type=f32) * weights
             inside = jnp.dot(s.astype(bf16), v, preferred_element_type=f32)
             carried = jnp.dot(q, state, preferred_element_type=f32) * jnp.exp(-rate * (steps + 1.0))
             out = inside + carried
-            mix[rows, cols] = out
+            mix[r * 8 + h] = out
             trail = k.astype(f32) * jnp.exp(-rate * (LANES - 1.0 - steps))
             high = trail.astype(bf16)
             low = (trail - high.astype(f32)).astype(bf16)
@@ -477,6 +575,26 @@
 
         a_cur[...] = a_buf[t]
 
+        def along_x(x, e):
+            spot = table[16 + 4 * x, e]
+            for z in range(1, 4):
+                spot = spot + table[16 + 4 * x + z, e]
+            return a_cur[spot]
+
+        for e in range(EXTRA):
+            for x in range(4):
+                xs_buf[t, x * EXTRA + e] = along_x(x, e)
+            xo_buf[t, px * EXTRA + e] = along_x(px, e)
+        for x in xs_to:
+            pltpu.make_async_remote_copy(
+                xs_buf.at[t, pl.ds(x * EXTRA, EXTRA)],
+                xo_buf.at[t, pl.ds(px * EXTRA, EXTRA)],
+                x_send.at[t],
+                x_recv.at[t],
+                device_id={"pool": x * 4 + pz},
+                device_id_type=MESH,
+            ).start()
+
         def pack(i, inner):
             for c in range(row_cap):
                 s_buf[slot, i * row_cap + c] = a_cur[table[i, c]]
@@ -484,20 +602,24 @@
 
         lax.fori_loop(0, 16, pack, 0)
         mine = pl.ds(pool * row_cap, row_cap)
-        for d in pools_to:
-            pltpu.make_async_remote_copy(
-                s_buf.at[slot, pl.ds(d * row_cap, row_cap)],
-                r_buf.at[t, mine],
-                b_send.at[slot],
-                b_recv.at[t],
-                device_id={"pool": d},
-                device_id_type=MESH,
-            ).start()
+        for first in range(0, row_cap, PIECE):
+            size = min(PIECE, row_cap - first)
+            for d in pools_to:
+                pltpu.make_async_remote_copy(
+                    s_buf.at[slot, pl.ds(d * row_cap + first, size)],
+                    r_buf.at[t, pl.ds(pool * row_cap + first, size)],
+                    b_send.at[slot],
+                    b_recv.at[t],
+                    device_id={"pool": d},
+                    device_id_type=MESH,
+                ).start()
         pltpu.make_async_copy(s_buf.at[slot, mine], r_buf.at[t, mine], keep_sems.at[slot]).start()
 
         @pl.when(t == 2)
         def _():
             wait_bytes(st_recv, st_sems.at[1])
+            for load in loads:
+                load.wait()
 
         @pl.when((t >= 2) & (t < 6))
         def _():
@@ -520,6 +642,21 @@
         def _():
             attend_chunk(t - 1)
 
+        wait_bytes(xo_buf.at[t, pl.ds(0, 3 * EXTRA)], x_recv.at[t])
+        xo_cur[...] = xo_buf[t]
+        for e in range(EXTRA):
+            for z in range(4):
+                zs_buf[t, z * EXTRA + e] = xo_cur[table[32 + px * 4 + z, e]]
+            r_buf[t, 16 * row_cap + pz * EXTRA + e] = xo_cur[table[32 + pool, e]]
+        for z in zs_to:
+            pltpu.make_async_remote_copy(
+                zs_buf.at[t, pl.ds(z * EXTRA, EXTRA)],
+                r_buf.at[t, pl.ds(16 * row_cap + pz * EXTRA, EXTRA)],
+                z_send.at[t],
+                z_recv.at[t],
+                device_id={"pool": px * 4 + z},
+                device_id_type=MESH,
+            ).start()
         return carry
 
     lax.fori_loop(0, CHUNKS, step, 0)
@@ -532,11 +669,20 @@
         factor = lax.rsqrt(squares / (64.0 * LANES) + 1e-06)
         column = jnp.broadcast_to(factor, (LANES, LANES)).T[:, :1]
         rows = rows_of(r)
-        gate = jax.nn.sigmoid(gate_in[rows, :].astype(f32))
-        light_out[rows, :] = (mix[rows, :] * column * gain_in[...] * gate).astype(bf16)
-        return carry
+
+        def one_head(h, inner):
+            cols = rows_of(h)
+            gate = jax.nn.sigmoid(gate_in[rows, cols].astype(f32))
+            light_out[rows, cols] = (mix[r * 8 + h] * column * gain_in[:, cols] * gate).astype(bf16)
+            return inner
+
+        return lax.fori_loop(0, 8, one_head, carry)
 
     lax.fori_loop(0, 4, finish_light, 0)
+    save_light = pltpu.make_async_copy(light_out, light_hbm, out_sems.at[0])
+    save_state = pltpu.make_async_copy(state_out, state_hbm, out_sems.at[1])
+    save_light.start()
+    save_state.start()
     attend_chunk(jnp.int32(CHUNKS - 1))
 
     def finish_soft(e, carry):
@@ -550,18 +696,23 @@
 
     def drain(t, carry):
         wait_bytes(a_buf.at[t, pl.ds(0, 112)], a_send.at[t])
+        wait_bytes(xs_buf.at[t, pl.ds(0, 3 * EXTRA)], x_send.at[t])
+        wait_bytes(zs_buf.at[t, pl.ds(0, 3 * EXTRA)], z_send.at[t])
         return carry
 
     lax.fori_loop(0, CHUNKS, drain, 0)
     wait_bytes(st_send.at[pl.ds(0, 15 * STATE_CAP)], st_sems.at[0])
     wait_bytes(sq_recv.at[pl.ds(0, 7)], sq_sems.at[0])
     wait_bytes(asked.at[pl.ds(0, 15)], ask_sems.at[0])
-
-
-def fused_call(row_cap, lengths, rates, wants, q, k, v, gate, gain, store, soft_q, pair, kv):
+    save_light.wait()
+    save_state.wait()
+
+
+def fused_call(row_cap, lengths, rates, wants, gain, q, k, v, gate, store, soft_q, pair, kv):
     tokens = LANES // CHUNKS
     bf16, f32 = jnp.bfloat16, jnp.float32
     vmem, smem = pl.BlockSpec(memory_space=pltpu.VMEM), pl.BlockSpec(memory_space=pltpu.SMEM)
+    hbm = pl.BlockSpec(memory_space=pl.ANY)
     dma = pltpu.SemaphoreType.DMA
     return pl.pallas_call(
         functools.partial(fused_kernel, row_cap),
@@ -569,21 +720,28 @@
             jax.ShapeDtypeStruct((512, 1024), bf16),
             jax.ShapeDtypeStruct((32, LANES, LANES), f32),
             jax.ShapeDtypeStruct((512, 1024), bf16),
-            jax.ShapeDtypeStruct((8, LANES), f32),
+            jax.ShapeDtypeStruct((1, 1), jnp.int32),
         ),
-        in_specs=[smem, smem] + [vmem] * 9 + [pl.BlockSpec(memory_space=pl.ANY)],
-        out_specs=(vmem, vmem, vmem, vmem),
+        in_specs=[smem, smem, vmem, vmem] + [hbm] * 8,
+        out_specs=(hbm, hbm, vmem, smem),
         scratch_shapes=[
+            pltpu.VMEM((512, 1024), bf16),
+            pltpu.VMEM((512, 1024), bf16),
+            pltpu.VMEM((512, 1024), bf16),
+            pltpu.VMEM((512, 1024), bf16),
+            pltpu.VMEM((512, 256), bf16),
+            pltpu.VMEM((512, 1024), bf16),
+            pltpu.VMEM((32, LANES, LANES), f32),
             pltpu.VMEM((CHUNKS, 128, tokens, 256), bf16),
             pltpu.VMEM((128, tokens, 256), bf16),
             pltpu.VMEM((2, 16 * row_cap, tokens, 256), bf16),
-            pltpu.VMEM((CHUNKS, 16 * row_cap, tokens, 256), bf16),
-            pltpu.VMEM((16 * row_cap, tokens, 256), bf16),
+            pltpu.VMEM((CHUNKS, 16 * row_cap + 4 * EXTRA, tokens, 256), bf16),
+            pltpu.VMEM((16 * row_cap + 4 * EXTRA, tokens, 256), bf16),
             pltpu.VMEM((32 * tokens, LANES), bf16),
             pltpu.VMEM((32 * tokens, LANES), bf16),
             pltpu.VMEM((16 * STATE_CAP, LANES, LANES), bf16),
             pltpu.VMEM((16 * STATE_CAP, LANES, LANES), bf16),
-            pltpu.VMEM((512, 1024), f32),
+            pltpu.VMEM((32, LANES, LANES), f32),
             pltpu.VMEM((4, 8, LANES), f32),
             pltpu.VMEM((8, 4, 8, LANES), f32),
             pltpu.VMEM((4, 1024, LANES), bf16),
@@ -594,19 +752,31 @@
             dma((2,)),
             dma((CHUNKS,)),
             dma((2,)),
+            pltpu.VMEM((CHUNKS, 4 * EXTRA, tokens, 256), bf16),
+            pltpu.VMEM((CHUNKS, 4 * EXTRA, tokens, 256), bf16),
+            pltpu.VMEM((4 * EXTRA, tokens, 256), bf16),
+            pltpu.VMEM((CHUNKS, 4 * EXTRA, tokens, 256), bf16),
+            dma((CHUNKS,)),
+            dma((CHUNKS,)),
+            dma((CHUNKS,)),
+            dma((CHUNKS,)),
             dma((2,)),
             dma((2,)),
             pltpu.VMEM((16, 8, LANES), jnp.int32),
-            pltpu.VMEM((40, LANES), jnp.int32),
-            pltpu.SMEM((40, LANES), jnp.int32),
+            pltpu.VMEM((24, LANES), jnp.int32),
+            pltpu.SMEM((24, LANES), jnp.int32),
+            pltpu.VMEM((56, LANES), jnp.int32),
+            pltpu.SMEM((56, LANES), jnp.int32),
             dma((2,)),
-            dma,
+            dma((2,)),
+            dma((7,)),
+            dma((2,)),
         ],
         compiler_params=pltpu.CompilerParams(
-            collective_id=1, has_side_effects=True, vmem_limit_bytes=60 * 2**20
+            collective_id=1, has_side_effects=True, vmem_limit_bytes=62 * 2**20
         ),
         cost_estimate=pl.CostEstimate(flops=10**10, bytes_accessed=3 * 10**7, transcendentals=2 * 10**7),
-    )(lengths, rates, wants, q, k, v, gate, gain, store, soft_q, pair, kv)
+    )(lengths, rates, wants, gain, q, k, v, gate, store, soft_q, pair, kv)
 
 
 def wanted(state_slot, page_holder, page_local, prefix_len):
@@ -638,11 +808,11 @@
         prefix_len,
         decay_rate,
         wanted(state_slot, page_holder, page_local, prefix_len),
+        norm_gain.reshape(1, -1),
         light_query,
         light_key,
         light_value,
         light_gate,
-        norm_gain.reshape(1, -1),
         state_store.reshape(32, LANES, LANES),
         soft_query,
         soft_pair,
@@ -670,7 +840,7 @@
             prefix_len,
         )
 
-    return lax.cond(crowd[0, 0] <= ROW_CAP, quick, general)
+    return lax.cond(crowd[0, 0] <= EXTRA, quick, general)
 
 
 def solution(mesh):

time: 199 us -> 173 us (0.87)
  Pallas kernels: 187 us -> 163 us
    pallas_call x1, Pallas kernels: 187 us -> 163 us  [fused_call(): pl.pallas_call(functools.partial(fused_kernel, row_cap), out_shape=(jax.S...]
    unnamed x21 -> x19, local copies, waits for them, and re-layouts: 5.38 us -> 5.37 us
where the time goes in v3:
time: 173 us
  Pallas kernels  163 us (94%)
  local copies, waits for them, and re-layouts  6.3 us (4%)
  other arithmetic  2.11 us (1%)
    pallas_call x1, Pallas kernels, fused_call(): pl.pallas_call(functools.partial(fused_kernel, row_cap), out_shape=(jax.S...  163 us
    unnamed x19, local copies, waits for them, and re-layouts  5.37 us

profile of v3, /device:TPU:1, one launch (start us, length us, event | category | flops | bytes accessed | tf_op | source)
XLA Modules:
  0.0 172.7 jit_solution(12857206803131289606)
XLA Ops:
  0.6 0.7 broadcast_multiply_fusion.2
  1.3 0.8 add_select_fusion.2
  2.1 0.1 reshape.674
  2.2 0.1 pad.9.clone
  2.2 0.8 reshape.675
  3.0 0.7 fusion.59.wants
  3.7 0.0 copy-start.5
  3.7 0.0 copy-start.7
  3.7 0.0 copy-start.10
  3.7 0.0 copy-start.12
  3.7 162.7 %shard_map.163 = (bf16[512,1024]{1,0:T(8,128)(2,1)}, f32[32,128,128]{2,1,0:T(8,128)}, bf16[512,1024]{1,0:T(8,128)(2,1)}, s32[1,1]{1,0:T(1,128)}) custom-call(s32[4]{0:T(128)} %lengths.1, f32[8]{0:T(128)} %rates.1, s32[8,128]{1,0:T(8,128)} %fusion.59.wants, f32[1,1024]{1,0:T(1,128)} %bitcast.143, bf16[512,1024]{1,0:T(8,128)(2,1)} %q_hbm.1, ...), custom_call_target="tpu_custom_call" | custom-call | flops 10000000000 | bytes 30000000 | tf_op jit(solution)/shard_map/pallas_call | solution.py:717
  167.1 0.0 copy-done.5
  167.1 0.0 copy-done.7
  167.1 0.0 copy-done.8
  167.1 0.0 copy-done.9
  167.1 0.0 copy-done.10
  167.1 0.0 copy-done.12
  167.1 0.2 conditional.1
  167.4 0.0 copy-start.3
  167.4 2.4 %copy.149 = bf16[512,1024]{1,0:T(8,128)(2,1)} copy(bf16[512,1024]{1,0:T(8,128)(2,1)} %get-tuple-element.384) | data formatting | bytes 2097152
  169.8 0.0 copy-done.3
  169.8 1.3 copy.150
  171.1 0.6 copy-done.6
  171.8 1.0 copy.151
  (5 shorter events, 0.0 us)
Async XLA Ops:
  3.7 163.4 %copy-start.5 = (bf16[512,1024]{1,0:T(8,128)(2,1)S(1)}, bf16[512,1024]{1,0:T(8,128)(2,1)}, u32[]{:S(2)}) copy-start(bf16[512,1024]{1,0:T(8,128)(2,1)} %k_hbm.1) | copy-start | bytes 3145732
  3.7 163.4 %copy-start.7 = (s32[4,8]{1,0:T(4,128)S(1)}, s32[4,8]{1,0:T(4,128)}, u32[]{:S(2)}) copy-start(s32[4,8]{1,0:T(4,128)} %param.25) | copy-start | bytes 388
  3.7 163.4 %copy-start.8 = (s32[4,32,1]{1,2,0:T(1,128)S(1)}, s32[4,32,1]{1,2,0:T(1,128)}, u32[]{:S(2)}) copy-start(s32[4,32,1]{1,2,0:T(1,128)} %param.29) | copy-start | bytes 1540
  3.7 163.4 %copy-start.9 = (s32[4,32]{1,0:T(4,128)S(1)}, s32[4,32]{1,0:T(4,128)}, u32[]{:S(2)}) copy-start(s32[4,32]{1,0:T(4,128)} %param.30) | copy-start | bytes 1540
  3.7 163.4 %copy-start.10 = (f32[1024]{0:T(1024)S(1)}, f32[1024]{0:T(1024)}, u32[]{:S(2)}) copy-start(f32[1024]{0:T(1024)} %param.23) | copy-start | bytes 12292
  3.7 163.4 %copy-start.12 = (f32[8]{0:T(128)S(1)}, f32[8]{0:T(128)}, u32[]{:S(2)}) copy-start(f32[8]{0:T(128)} %rates.1) | copy-start | bytes 100
  167.4 2.4 %copy-start.3 = (f32[4,8,128,128]{3,2,1,0:T(8,128)S(1)}, f32[4,8,128,128]{3,2,1,0:T(8,128)}, u32[]{:S(2)}) copy-start(f32[4,8,128,128]{3,2,1,0:T(8,128)} %get-tuple-element.385) | copy-start | bytes 6291460
  169.8 2.0 %copy-start.6 = (bf16[512,1024]{1,0:T(8,128)(2,1)S(1)}, bf16[512,1024]{1,0:T(8,128)(2,1)}, u32[]{:S(2)}) copy-start(bf16[512,1024]{1,0:T(8,128)(2,1)} %get-tuple-element.386) | copy-start | bytes 3145732

commit v4 on v3

--- a/solution.py
+++ b/solution.py
@@ -210,6 +210,9 @@
 EXTRA = 6
 STATE_CAP = 4
 PIECE = 4
+STATE_PIECE = 1
+LAG = 2
+SLOTS = 2
 LOG2E = 1.4426950408889634
 
 
@@ -312,7 +315,9 @@
     row_cap,
     lengths,
     rates,
-    wants,
+    page_holder,
+    page_local,
+    state_slot,
     gain_in,
     q_hbm,
     k_hbm,
@@ -352,7 +357,6 @@
     a_recv,
     b_send,
     b_recv,
-    keep_sems,
     xs_buf,
     xo_buf,
     xo_cur,
@@ -363,6 +367,7 @@
     z_recv,
     st_sems,
     sq_sems,
+    wants,
     asked,
     st_lists,
     st_table,
@@ -404,6 +409,13 @@
         ).start()
         return carry
 
+    page_start = lax.broadcasted_iota(jnp.int32, (1, 32), 1) * LANES
+    wants[...] = jnp.full((8, LANES), 4095, jnp.int32)
+    for r in range(4):
+        ids = page_holder[r : r + 1, :] * 16 + page_local[r : r + 1, :]
+        wants[0:1, r * 32 : r * 32 + 32] = jnp.where(page_start < lengths[r], ids, 4095)
+        wants[1:2, r * 8 : r * 8 + 8] = state_slot[r : r + 1, :]
+
     barrier = pltpu.get_barrier_semaphore()
     for d in heads_to:
         pl.semaphore_signal(barrier, inc=1, device_id={"head": d}, device_id_type=MESH)
@@ -459,22 +471,22 @@
 
     lax.fori_loop(0, 16, pack_state, 0)
     mine_st = pl.ds(pool * STATE_CAP, STATE_CAP)
-    for d in pools_to:
-        pltpu.make_async_remote_copy(
-            st_send.at[pl.ds(d * STATE_CAP, STATE_CAP)],
-            st_recv.at[mine_st],
-            st_sems.at[0],
-            st_sems.at[1],
-            device_id={"pool": d},
-            device_id_type=MESH,
-        ).start()
+    for first in range(0, STATE_CAP, STATE_PIECE):
+        for d in pools_to:
+            pltpu.make_async_remote_copy(
+                st_send.at[pl.ds(d * STATE_CAP + first, STATE_PIECE)],
+                st_recv.at[pl.ds(pool * STATE_CAP + first, STATE_PIECE)],
+                st_sems.at[0],
+                st_sems.at[1],
+                device_id={"pool": d},
+                device_id_type=MESH,
+            ).start()
     pltpu.make_async_copy(st_send.at[mine_st], st_recv.at[mine_st], st_sems.at[1]).start()
-
-    lax.fori_loop(2, CHUNKS, send_store, 0)
 
     page_lists(row_cap, pool, wants, asked, lists)
     to_table = pltpu.make_async_copy(lists, table, list_sems.at[1])
     to_table.start()
+    lax.fori_loop(2, CHUNKS, send_store, 0)
     to_table.wait()
     crowd_out[0, 0] = table[49, 0]
 
@@ -496,15 +508,11 @@
         top[r, rows_of(h), :] = jnp.broadcast_to(peak, (LANES, LANES))
         return carry
 
-    load_pair.wait()
-    wait_bytes(q_cat, in_sems.at[6])
-    lax.fori_loop(0, 32, open_softmax, 0)
 
     lane = lax.broadcasted_iota(jnp.int32, (1, keys), 1)
 
     def attend_chunk(t):
         wait_bytes(r_buf.at[t, pl.ds(0, 15 * row_cap)], b_recv.at[t])
-        wait_bytes(r_buf.at[t, pl.ds(0, row_cap)], keep_sems.at[lax.rem(t, 2)])
         wait_bytes(r_buf.at[t, pl.ds(0, 3 * EXTRA)], z_recv.at[t])
         r_cur[...] = r_buf[t]
         spot = (lane // tokens) * LANES + t * tokens + lax.rem(lane, tokens)
@@ -565,11 +573,11 @@
         total = lax.fori_loop(0, 8, one_head, jnp.zeros((LANES, 1), f32))
         sq_send[r] = jnp.broadcast_to(total, (LANES, LANES)).T[:8, :]
 
-    def step(t, carry):
+    def send_chunk(t):
         wait_bytes(a_buf.at[t], a_recv.at[t])
-        slot = lax.rem(t, 2)
-
-        @pl.when(t >= 2)
+        slot = lax.rem(t, SLOTS)
+
+        @pl.when(t >= SLOTS)
         def _():
             wait_bytes(s_buf.at[slot, pl.ds(0, 15 * row_cap)], b_send.at[slot])
 
@@ -601,7 +609,6 @@
             return inner
 
         lax.fori_loop(0, 16, pack, 0)
-        mine = pl.ds(pool * row_cap, row_cap)
         for first in range(0, row_cap, PIECE):
             size = min(PIECE, row_cap - first)
             for d in pools_to:
@@ -613,35 +620,10 @@
                     device_id={"pool": d},
                     device_id_type=MESH,
                 ).start()
-        pltpu.make_async_copy(s_buf.at[slot, mine], r_buf.at[t, mine], keep_sems.at[slot]).start()
-
-        @pl.when(t == 2)
-        def _():
-            wait_bytes(st_recv, st_sems.at[1])
-            for load in loads:
-                load.wait()
-
-        @pl.when((t >= 2) & (t < 6))
-        def _():
-            light_request(t - 2)
-
-        @pl.when(t == 6)
-        def _():
-            sq_recv[head] = sq_send[...]
-            for d in heads_to:
-                pltpu.make_async_remote_copy(
-                    sq_send,
-                    sq_recv.at[head],
-                    sq_sems.at[0],
-                    sq_sems.at[1],
-                    device_id={"head": d},
-                    device_id_type=MESH,
-                ).start()
-
-        @pl.when(t >= 1)
-        def _():
-            attend_chunk(t - 1)
-
+        for c in range(row_cap):
+            r_buf[t, pool * row_cap + c] = a_cur[table[pool, c]]
+
+    def relay_chunk(t):
         wait_bytes(xo_buf.at[t, pl.ds(0, 3 * EXTRA)], x_recv.at[t])
         xo_cur[...] = xo_buf[t]
         for e in range(EXTRA):
@@ -657,12 +639,7 @@
                 device_id={"pool": px * 4 + z},
                 device_id_type=MESH,
             ).start()
-        return carry
-
-    lax.fori_loop(0, CHUNKS, step, 0)
-    for slot in range(2):
-        wait_bytes(s_buf.at[slot, pl.ds(0, 15 * row_cap)], b_send.at[slot])
-    wait_bytes(sq_recv.at[pl.ds(0, 7)], sq_sems.at[1])
+
 
     def finish_light(r, carry):
         squares = jnp.sum(sq_recv[:, r, :1, :], axis=0)
@@ -678,12 +655,62 @@
 
         return lax.fori_loop(0, 8, one_head, carry)
 
-    lax.fori_loop(0, 4, finish_light, 0)
     save_light = pltpu.make_async_copy(light_out, light_hbm, out_sems.at[0])
     save_state = pltpu.make_async_copy(state_out, state_hbm, out_sems.at[1])
-    save_light.start()
-    save_state.start()
-    attend_chunk(jnp.int32(CHUNKS - 1))
+
+    def step(t, carry):
+        @pl.when(t < CHUNKS)
+        def _():
+            send_chunk(t)
+
+        @pl.when(t == 0)
+        def _():
+            load_pair.wait()
+            wait_bytes(q_cat, in_sems.at[6])
+            lax.fori_loop(0, 32, open_softmax, 0)
+
+        @pl.when((t >= 1) & (t <= CHUNKS))
+        def _():
+            relay_chunk(t - 1)
+
+        @pl.when(t == 2)
+        def _():
+            wait_bytes(st_recv, st_sems.at[1])
+            for load in loads:
+                load.wait()
+
+        @pl.when((t >= 2) & (t < 6))
+        def _():
+            light_request(t - 2)
+
+        @pl.when(t == 6)
+        def _():
+            sq_recv[head] = sq_send[...]
+            for d in heads_to:
+                pltpu.make_async_remote_copy(
+                    sq_send,
+                    sq_recv.at[head],
+                    sq_sems.at[0],
+                    sq_sems.at[1],
+                    device_id={"head": d},
+                    device_id_type=MESH,
+                ).start()
+
+        @pl.when(t == CHUNKS)
+        def _():
+            wait_bytes(sq_recv.at[pl.ds(0, 7)], sq_sems.at[1])
+            lax.fori_loop(0, 4, finish_light, 0)
+            save_light.start()
+            save_state.start()
+
+        @pl.when(t >= LAG)
+        def _():
+            attend_chunk(t - LAG)
+
+        return carry
+
+
+    lax.fori_loop(0, CHUNKS + LAG, step, 0)
 
     def finish_soft(e, carry):
         r, h = e // 8, lax.rem(e, 8)
@@ -701,6 +728,8 @@
         return carry
 
     lax.fori_loop(0, CHUNKS, drain, 0)
+    for slot in range(SLOTS):
+        wait_bytes(s_buf.at[slot, pl.ds(0, 15 * row_cap)], b_send.at[slot])
     wait_bytes(st_send.at[pl.ds(0, 15 * STATE_CAP)], st_sems.at[0])
     wait_bytes(sq_recv.at[pl.ds(0, 7)], sq_sems.at[0])
     wait_bytes(asked.at[pl.ds(0, 15)], ask_sems.at[0])
@@ -708,7 +737,7 @@
     save_state.wait()
 
 
-def fused_call(row_cap, lengths, rates, wants, gain, q, k, v, gate, store, soft_q, pair, kv):
+def fused_call(row_cap, lengths, rates, page_holder, page_local, state_slot, gain, q, k, v, gate, store, soft_q, pair, kv):
     tokens = LANES // CHUNKS
     bf16, f32 = jnp.bfloat16, jnp.float32
     vmem, smem = pl.BlockSpec(memory_space=pltpu.VMEM), pl.BlockSpec(memory_space=pltpu.SMEM)
@@ -722,7 +751,7 @@
             jax.ShapeDtypeStruct((512, 1024), bf16),
             jax.ShapeDtypeStruct((1, 1), jnp.int32),
         ),
-        in_specs=[smem, smem, vmem, vmem] + [hbm] * 8,
+        in_specs=[smem, smem, vmem, vmem, vmem, vmem] + [hbm] * 8,
         out_specs=(hbm, hbm, vmem, smem),
         scratch_shapes=[
             pltpu.VMEM((512, 1024), bf16),
@@ -734,7 +763,7 @@
             pltpu.VMEM((32, LANES, LANES), f32),
             pltpu.VMEM((CHUNKS, 128, tokens, 256), bf16),
             pltpu.VMEM((128, tokens, 256), bf16),
-            pltpu.VMEM((2, 16 * row_cap, tokens, 256), bf16),
+            pltpu.VMEM((SLOTS, 16 * row_cap, tokens, 256), bf16),
             pltpu.VMEM((CHUNKS, 16 * row_cap + 4 * EXTRA, tokens, 256), bf16),
             pltpu.VMEM((16 * row_cap + 4 * EXTRA, tokens, 256), bf16),
             pltpu.VMEM((32 * tokens, LANES), bf16),
@@ -749,9 +778,8 @@
             pltpu.VMEM((4, 1024, LANES), f32),
             dma((CHUNKS,)),
             dma((CHUNKS,)),
-            dma((2,)),
+            dma((SLOTS,)),
             dma((CHUNKS,)),
-            dma((2,)),
             pltpu.VMEM((CHUNKS, 4 * EXTRA, tokens, 256), bf16),
             pltpu.VMEM((CHUNKS, 4 * EXTRA, tokens, 256), bf16),
             pltpu.VMEM((4 * EXTRA, tokens, 256), bf16),
@@ -762,6 +790,7 @@
             dma((CHUNKS,)),
             dma((2,)),
             dma((2,)),
+            pltpu.VMEM((8, LANES), jnp.int32),
             pltpu.VMEM((16, 8, LANES), jnp.int32),
             pltpu.VMEM((24, LANES), jnp.int32),
             pltpu.SMEM((24, LANES), jnp.int32),
@@ -773,18 +802,34 @@
             dma((2,)),
         ],
         compiler_params=pltpu.CompilerParams(
-            collective_id=1, has_side_effects=True, vmem_limit_bytes=62 * 2**20
+            collective_id=1, has_side_effects=True, vmem_limit_bytes=63 * 2**20
         ),
         cost_estimate=pl.CostEstimate(flops=10**10, bytes_accessed=3 * 10**7, transcendentals=2 * 10**7),
-    )(lengths, rates, wants, gain, q, k, v, gate, store, soft_q, pair, kv)
-
-
-def wanted(state_slot, page_holder, page_local, prefix_len):
-    pages = page_holder[:, :, 0] * 16 + page_local
-    active = jnp.arange(32)[None, :] * LANES < prefix_len[:, None]
-    own_pages = jnp.where(active, pages, 4095).reshape(1, -1)
-    own_states = jnp.pad(state_slot.reshape(1, -1), ((0, 0), (0, 96)), constant_values=255)
-    return jnp.concatenate([own_pages, own_states, jnp.zeros((6, LANES), jnp.int32)]).astype(jnp.int32)
+    )(lengths, rates, page_holder, page_local, state_slot, gain, q, k, v, gate, store, soft_q, pair, kv)
+
+
+def keep_kernel(*refs):
+    half = len(refs) // 2
+    for n in range(half):
+        refs[half + n][...] = refs[n][...]
+
+
+def keep_results(*arrays):
+    steps = 4
+    specs = [
+        pl.BlockSpec(
+            (x.shape[0] // steps,) + x.shape[1:], lambda i, rank=x.ndim: (i,) + (0,) * (rank - 1)
+        )
+        for x in arrays
+    ]
+    return pl.pallas_call(
+        keep_kernel,
+        grid=(steps,),
+        out_shape=tuple(jax.ShapeDtypeStruct(x.shape, x.dtype) for x in arrays),
+        in_specs=specs,
+        out_specs=tuple(specs),
+        compiler_params=pltpu.CompilerParams(vmem_limit_bytes=16 * 2**20),
+    )(*arrays)
 
 
 def body(
@@ -807,7 +852,9 @@
         ROW_CAP,
         prefix_len,
         decay_rate,
-        wanted(state_slot, page_holder, page_local, prefix_len),
+        page_holder.reshape(4, 32),
+        page_local,
+        state_slot,
         norm_gain.reshape(1, -1),
         light_query,
         light_key,
@@ -820,7 +867,8 @@
     )
 
     def quick():
-        return light, states.reshape(4, 8, LANES, LANES), soft
+        kept = keep_results(light, states, soft)
+        return kept[0], kept[1].reshape(4, 8, LANES, LANES), kept[2]
 
     def general():
         return general_body(

time: 173 us -> 162 us (0.936)
  local copies, waits for them, and re-layouts: 6.3 us -> 0.02 us
  Pallas kernels: 163 us -> 159 us
  other arithmetic: 2.11 us -> 0 us
    pallas_call x1, Pallas kernels: 163 us -> 154 us  [fused_call(): pl.pallas_call(functools.partial(fused_kernel, row_cap), out_shape=(jax.S...]
    unnamed x19 -> x10, local copies, waits for them, and re-layouts: 5.37 us -> 0.02 us
    pallas_call x0 -> x1, Pallas kernels: none -> 4.66 us  [keep_results(): pl.pallas_call(keep_kernel, grid=(steps,), out_shape=tuple((jax.ShapeDtyp...]
where the time goes in v4:
time: 162 us; the launch traced here: 161 us
  Pallas kernels  159 us (98%)
    pallas_call x1, Pallas kernels, fused_call(): pl.pallas_call(functools.partial(fused_kernel, row_cap), out_shape=(jax.S...  154 us
    pallas_call x1, Pallas kernels, keep_results(): pl.pallas_call(keep_kernel, grid=(steps,), out_shape=tuple((jax.ShapeDtyp...  4.66 us

profile of v4, /device:TPU:1, one launch (start us, length us, event | category | flops | bytes accessed | tf_op | source)
XLA Modules:
  0.0 160.6 jit_solution(7478465735199104828)
XLA Ops:
  0.6 0.0 copy-start.5
  0.6 0.0 copy-start.6
  0.7 0.0 copy-start.7
  0.7 0.0 copy-start.8
  0.7 0.0 copy-start.10
  0.7 154.3 %shard_map.163 = (bf16[512,1024]{1,0:T(8,128)(2,1)}, f32[32,128,128]{2,1,0:T(8,128)}, bf16[512,1024]{1,0:T(8,128)(2,1)}, s32[1,1]{1,0:T(1,128)}) custom-call(s32[4]{0:T(128)} %lengths.1, f32[8]{0:T(128)} %rates.1, s32[4,32]{1,0:T(4,128)} %bitcast.137, s32[4,32]{1,0:T(4,128)} %page_local.1, s32[4,8]{1,0:T(4,128)} %state_slot.1, f32[1,1024]{1,0:T(1,128)} %bitcast.142, ...), custom_call_target="tpu_custom_call" | custom-call | flops 10000000000 | bytes 30000000 | tf_op jit(solution)/shard_map/pallas_call | solution.py:746
  155.7 0.0 copy-done.5
  155.7 0.0 copy-done.6
  155.7 0.0 copy-done.7
  155.7 0.0 copy-done.8
  155.7 0.0 copy-done.10
  155.7 4.9 %conditional.1 = (bf16[512,1024]{1,0:T(8,128)(2,1)}, f32[4,8,128,128]{3,2,1,0:T(8,128)}, bf16[512,1024]{1,0:T(8,128)(2,1)}) conditional(s32[]{:T(128)} %bitcast.38, (bf16[512,1024]{1,0:T(8,128)(2,1)}, bf16[512,1024]{1,0:T(8,128)(2,1)}, f32[8]{0:T(128)S(1)}, bf16[512,1024]{1,0:T(8,128)(2,1)}, s32[4,8]{1,0:T(4,128)S(1)}, ...), branch_computations={%region_0.13_spmd, %region_13.14_spmd} | conditional | flops 4164528640 | bytes 313803552 | solution.py:891
  156.0 4.7 %branch_1_fun.1 = (bf16[512,1024]{1,0:T(8,128)(2,1)}, f32[32,128,128]{2,1,0:T(8,128)}, bf16[512,1024]{1,0:T(8,128)(2,1)}) custom-call(bf16[512,1024]{1,0:T(8,128)(2,1)} %get-tuple-element.154.refs_0_, f32[32,128,128]{2,1,0:T(8,128)} %get-tuple-element.155.refs_1_, bf16[512,1024]{1,0:T(8,128)(2,1)} %get-tuple-element.156.refs_2_), custom_call_target="tpu_custom_call" | custom-call | tf_op jit(solution)/shard_map/cond/branch_1_fun/pallas_call | solution.py:825
Async XLA Ops:
  0.6 155.1 %copy-start.5 = (s32[4,32,1]{1,2,0:T(1,128)S(1)}, s32[4,32,1]{1,2,0:T(1,128)}, u32[]{:S(2)}) copy-start(s32[4,32,1]{1,2,0:T(1,128)} %param.29) | copy-start | bytes 1540
  0.6 155.1 %copy-start.6 = (s32[4,8]{1,0:T(4,128)S(1)}, s32[4,8]{1,0:T(4,128)}, u32[]{:S(2)}) copy-start(s32[4,8]{1,0:T(4,128)} %state_slot.1) | copy-start | bytes 388
  0.7 155.1 %copy-start.7 = (f32[1024]{0:T(1024)S(1)}, f32[1024]{0:T(1024)}, u32[]{:S(2)}) copy-start(f32[1024]{0:T(1024)} %param.23) | copy-start | bytes 12292
  0.7 155.1 %copy-start.8 = (s32[4,32]{1,0:T(4,128)S(1)}, s32[4,32]{1,0:T(4,128)}, u32[]{:S(2)}) copy-start(s32[4,32]{1,0:T(4,128)} %page_local.1) | copy-start | bytes 1540
  0.7 155.1 %copy-start.10 = (f32[8]{0:T(128)S(1)}, f32[8]{0:T(128)}, u32[]{:S(2)}) copy-start(f32[8]{0:T(128)} %rates.1) | copy-start | bytes 100

commit v5 on v4

--- a/solution.py
+++ b/solution.py
@@ -387,7 +387,11 @@
     heads_to = [lax.rem(hy + k // 2, 4) * 2 + lax.rem(hc + k % 2, 2) for k in range(1, 8)]
     xs_to = [lax.rem(px + k, 4) for k in range(1, 4)]
     zs_to = [lax.rem(pz + k, 4) for k in range(1, 4)]
-    pools_to = [lax.rem(px + k // 4, 4) * 4 + lax.rem(pz + k % 4, 4) for k in range(1, 16)]
+    turn = (1 + 2 * hc)
+    pools_to = [
+        lax.rem(px + dx * turn, 4) * 4 + lax.rem(pz + dz * turn, 4)
+        for dx, dz in [(2, 2), (1, 2), (2, 1), (3, 2), (2, 3), (1, 1), (3, 3), (1, 3), (3, 1), (2, 0), (0, 2), (1, 0), (0, 1), (3, 0), (0, 3)]
+    ]
 
     def rows_of(r):
         return pl.ds(pl.multiple_of(r * LANES, LANES), LANES)
@@ -815,7 +819,7 @@
 
 
 def keep_results(*arrays):
-    steps = 4
+    steps = 8
     specs = [
         pl.BlockSpec(
             (x.shape[0] // steps,) + x.shape[1:], lambda i, rank=x.ndim: (i,) + (0,) * (rank - 1)

time: 162 us -> 164 us (1.012)
  Pallas kernels: 159 us -> 162 us
    pallas_call x1, Pallas kernels: 4.66 us -> 6.54 us  [keep_results(): pl.pallas_call(keep_kernel, grid=(steps,), out_shape=tuple((jax.ShapeDtyp...]
where the time goes in v5:
time: 164 us
  Pallas kernels  162 us (99%)
    pallas_call x1, Pallas kernels, fused_call(): pl.pallas_call(functools.partial(fused_kernel, row_cap), out_shape=(jax.S...  155 us
    pallas_call x1, Pallas kernels, keep_results(): pl.pallas_call(keep_kernel, grid=(steps,), out_shape=tuple((jax.ShapeDtyp...  6.54 us

profile of v5, /device:TPU:1, one launch (start us, length us, event | category | flops | bytes accessed | tf_op | source)
XLA Modules:
  0.0 163.5 jit_solution(14590329826286900825)
XLA Ops:
  0.6 0.0 copy-start.5
  0.6 0.0 copy-start.6
  0.7 0.0 copy-start.7
  0.7 0.0 copy-start.8
  0.7 0.0 copy-start.10
  0.7 155.3 %shard_map.163 = (bf16[512,1024]{1,0:T(8,128)(2,1)}, f32[32,128,128]{2,1,0:T(8,128)}, bf16[512,1024]{1,0:T(8,128)(2,1)}, s32[1,1]{1,0:T(1,128)}) custom-call(s32[4]{0:T(128)} %lengths.1, f32[8]{0:T(128)} %rates.1, s32[4,32]{1,0:T(4,128)} %bitcast.137, s32[4,32]{1,0:T(4,128)} %page_local.1, s32[4,8]{1,0:T(4,128)} %state_slot.1, f32[1,1024]{1,0:T(1,128)} %bitcast.142, ...), custom_call_target="tpu_custom_call" | custom-call | flops 10000000000 | bytes 30000000 | tf_op jit(solution)/shard_map/pallas_call | solution.py:750
  156.7 0.0 copy-done.5
  156.7 0.0 copy-done.6
  156.7 0.0 copy-done.7
  156.7 0.0 copy-done.8
  156.7 0.0 copy-done.10
  156.7 6.8 %conditional.1 = (bf16[512,1024]{1,0:T(8,128)(2,1)}, f32[4,8,128,128]{3,2,1,0:T(8,128)}, bf16[512,1024]{1,0:T(8,128)(2,1)}) conditional(s32[]{:T(128)} %bitcast.38, (bf16[512,1024]{1,0:T(8,128)(2,1)}, bf16[512,1024]{1,0:T(8,128)(2,1)}, f32[8]{0:T(128)S(1)}, bf16[512,1024]{1,0:T(8,128)(2,1)}, s32[4,8]{1,0:T(4,128)S(1)}, ...), branch_computations={%region_0.13_spmd, %region_13.14_spmd} | conditional | flops 4164528640 | bytes 313803552 | solution.py:895
  157.0 6.5 %branch_1_fun.1 = (bf16[512,1024]{1,0:T(8,128)(2,1)}, f32[32,128,128]{2,1,0:T(8,128)}, bf16[512,1024]{1,0:T(8,128)(2,1)}) custom-call(bf16[512,1024]{1,0:T(8,128)(2,1)} %get-tuple-element.154.refs_0_, f32[32,128,128]{2,1,0:T(8,128)} %get-tuple-element.155.refs_1_, bf16[512,1024]{1,0:T(8,128)(2,1)} %get-tuple-element.156.refs_2_), custom_call_target="tpu_custom_call" | custom-call | tf_op jit(solution)/shard_map/cond/branch_1_fun/pallas_call | solution.py:829
Async XLA Ops:
  0.6 156.0 %copy-start.5 = (s32[4,32,1]{1,2,0:T(1,128)S(1)}, s32[4,32,1]{1,2,0:T(1,128)}, u32[]{:S(2)}) copy-start(s32[4,32,1]{1,2,0:T(1,128)} %param.29) | copy-start | bytes 1540
  0.6 156.0 %copy-start.6 = (s32[4,8]{1,0:T(4,128)S(1)}, s32[4,8]{1,0:T(4,128)}, u32[]{:S(2)}) copy-start(s32[4,8]{1,0:T(4,128)} %state_slot.1) | copy-start | bytes 388
  0.7 156.0 %copy-start.7 = (f32[1024]{0:T(1024)S(1)}, f32[1024]{0:T(1024)}, u32[]{:S(2)}) copy-start(f32[1024]{0:T(1024)} %param.23) | copy-start | bytes 12292
  0.7 156.0 %copy-start.8 = (s32[4,32]{1,0:T(4,128)S(1)}, s32[4,32]{1,0:T(4,128)}, u32[]{:S(2)}) copy-start(s32[4,32]{1,0:T(4,128)} %page_local.1) | copy-start | bytes 1540
  0.7 156.0 %copy-start.10 = (f32[8]{0:T(128)S(1)}, f32[8]{0:T(128)}, u32[]{:S(2)}) copy-start(f32[8]{0:T(128)} %rates.1) | copy-start | bytes 100
